TPU v7x, 32 devices: a whole 2x2x4 slice. The times are simulated.
32 devices in a mesh: tm: 8 (over y, x, core), height: 4 (over z).
Axes of the slice: x: 2, y: 2, z: 4, core: 2. Of those that a mesh axis runs over, the one named last changes fastest.
Arguments:
- tokens: bfloat16 [16, 16, 80, 3072], P('tm', 'height'), may hold values from -6 to 6
- mod_scale: float32 [3072], replicated, may hold values from -3 to 3
- mod_shift: float32 [3072], replicated, may hold values from -3 to 3
- w_qkv: bfloat16 [3072, 4608], P(('tm', 'height')), may hold values from -0.109375 to 0.109375
- q_gain: float32 [128], replicated, may hold values from 0.25 to 1.75
- k_gain: float32 [128], replicated, may hold values from 0.25 to 1.75
- window: int32 [12, 3], replicated, may hold values from 0 to 2, as said below
- valid: int32 [16, 16, 80], replicated, may hold values from 0 to 1, as said below
Outputs:
- attended: bfloat16 [16, 16, 80, 1536], P('tm', 'height')
Inputs may be any that keep to these rules, and one draw needn't show every extreme that they name: `window`: column 0 is at most 1, column 1 at most 1, column 2 at most 2; some head has all three at these most values. `valid`: the last frames, rows and columns of the grid may be padding with 0; scattered tokens elsewhere are 0 too.
All inputs are finite; a program needn't handle non-finite values.
Results may differ from a plain program's by a relative error of at most 0.0055.
Values may be sent and summed in bfloat16 or wider, within the bound.
No kernel may reach another device: no remote copies, remote signals or barrier semaphores. Data moves between devices by JAX's collectives and lax.ppermute only.
A program may use at most 128 MiB of HBM per device.

v0:
```python
import jax
import jax.numpy as jnp
from jax import lax
from jax.sharding import PartitionSpec as P

HDIM = 128
HEADS = 12
TT = 1
TH = 2
TW = 8


EPS = 1e-06


def with_halo(cells, sides, width):
    for axis, dim in sides:
        count = lax.axis_size(axis)
        ends = count - 1
        head = lax.slice_in_dim(cells, 0, width, axis=dim)
        tail = lax.slice_in_dim(cells, cells.shape[dim] - width, cells.shape[dim], axis=dim)
        cells = jnp.concatenate(
            [
                lax.ppermute(tail, axis, [(i, (i + 1) % count) for i in range(ends)]),
                cells,
                lax.ppermute(head, axis, [((i + 1) % count, i) for i in range(ends)]),
            ],
            axis=dim,
        )
    return cells


def modulate(tokens, mod_scale, mod_shift):
    values = tokens.astype(jnp.float32)
    mean = jnp.mean(values, axis=-1, keepdims=True)
    centred = values - mean
    variance = jnp.mean(centred * centred, axis=-1, keepdims=True)
    normed = centred * lax.rsqrt(variance + EPS)
    return (normed * (1.0 + mod_scale) + mod_shift).astype(jnp.bfloat16)


def head_norm(values, gain):
    power = jnp.mean(values * values, axis=-1, keepdims=True)
    return (values * lax.rsqrt(power + EPS) * gain).astype(jnp.bfloat16)


def tile_coords(frames, rows, width):
    shape = (frames.shape[0], rows.shape[0], width)
    columns = jnp.arange(width, dtype=jnp.int32)
    frame_tiles = jnp.broadcast_to((frames // TT)[:, None, None], shape).reshape(-1)
    row_tiles = jnp.broadcast_to((rows // TH)[None, :, None], shape).reshape(-1)
    column_tiles = jnp.broadcast_to((columns // TW)[None, None, :], shape).reshape(-1)
    return (frame_tiles, row_tiles, column_tiles)


def per_device(tokens, mod_scale, mod_shift, w_qkv, q_gain, k_gain, window, valid):
    frame_count, row_count, width, features = tokens.shape
    token_count = frame_count * row_count * width
    modulated = modulate(tokens.reshape(token_count, features), mod_scale, mod_shift)
    full_weight = lax.all_gather(w_qkv, ("tm", "height"), axis=0, tiled=True)
    qkv = jnp.dot(modulated, full_weight, preferred_element_type=jnp.float32)
    inner = qkv.shape[1] // 3
    query = head_norm(qkv[:, :inner].reshape(token_count, HEADS, HDIM), q_gain)
    key = head_norm(qkv[:, inner : 2 * inner].reshape(token_count, HEADS, HDIM), k_gain)
    value = qkv[:, 2 * inner :].astype(jnp.bfloat16)
    tiled = (frame_count // TT, TT, row_count // TH, TH, width, inner)
    stacked = jnp.stack([key.reshape(tiled), value.reshape(tiled)])
    extended = with_halo(stacked, (("tm", 1), ("height", 3)), 1)
    frames_ext = frame_count + 2 * TT
    rows_ext = row_count + 2 * TH
    key_count = frames_ext * rows_ext * width
    extended = extended.reshape(2, key_count, HEADS, HDIM)
    key_heads = jnp.transpose(extended[0], (1, 0, 2))
    value_heads = jnp.transpose(extended[1], (1, 0, 2))
    query_heads = jnp.transpose(query, (1, 0, 2))
    frame_block = lax.axis_index("tm")
    row_block = lax.axis_index("height")
    first_frame = frame_block * frame_count
    first_row = row_block * row_count
    zero = jnp.int32(0)
    valid_pad = jnp.pad(valid, ((TT, TT), (TH, TH), (0, 0)))
    key_valid = (
        lax.dynamic_slice(
            valid_pad, (first_frame, first_row, zero), (frames_ext, rows_ext, width)
        ).reshape(-1)
        > 0
    )
    query_valid = (
        lax.dynamic_slice(
            valid, (first_frame, first_row, zero), (frame_count, row_count, width)
        ).reshape(-1)
        > 0
    )
    query_coords = tile_coords(
        first_frame + jnp.arange(frame_count, dtype=jnp.int32),
        first_row + jnp.arange(row_count, dtype=jnp.int32),
        width,
    )
    key_coords = tile_coords(
        first_frame - TT + jnp.arange(frames_ext, dtype=jnp.int32),
        first_row - TH + jnp.arange(rows_ext, dtype=jnp.int32),
        width,
    )
    apart_t, apart_h, apart_w = (
        jnp.abs(qa[:, None] - ka[None, :]) for qa, ka in zip(query_coords, key_coords)
    )
    seen = key_valid[None, :]
    scale = 1.0 / jnp.sqrt(jnp.float32(HDIM))

    def per_head(inputs):
        query_one, key_one, value_one, reach = inputs
        allowed = (apart_t <= reach[0]) & (apart_h <= reach[1]) & (apart_w <= reach[2]) & seen
        scores = (
            jnp.einsum("qd,kd->qk", query_one, key_one, preferred_element_type=jnp.float32) * scale
        )
        terms = jnp.where(allowed, jnp.exp(scores), jnp.float32(0.0))
        total = jnp.sum(terms, axis=-1, keepdims=True)
        total = jnp.where(query_valid[:, None], total, jnp.float32(1.0))
        weights = (terms / total).astype(jnp.bfloat16)
        result = jnp.dot(weights, value_one, preferred_element_type=jnp.float32)
        return jnp.where(query_valid[:, None], result, jnp.float32(0.0)).astype(jnp.bfloat16)

    heads_out = lax.map(per_head, (query_heads, key_heads, value_heads, window))
    attended = jnp.transpose(heads_out, (1, 0, 2)).reshape(frame_count, row_count, width, inner)
    return attended


def solution(mesh):
    in_specs = (
        P("tm", "height", None, None),
        P(),
        P(),
        P(("tm", "height"), None),
        P(),
        P(),
        P(),
        P(),
    )
    out_specs = P("tm", "height", None, None)
    return jax.shard_map(
        per_device, mesh=mesh, in_specs=in_specs, out_specs=out_specs, check_vma=False
    )
```

profile of v0, /device:TPU:4, one launch (start us, length us, event | category | flops | bytes accessed | tf_op | source)
XLA Modules:
  0.0 589.5 jit_solution(16271200248019554560)
XLA Ops:
  7.3 2.7 convert_reduce_fusion
  10.1 3.3 multiply_reduce_fusion
  13.5 4.9 fusion.25
  18.4 162.7 %all-gather.2.cloned.1.call-done = bf16[3072,4608]{1,0:T(8,128)(2,1)} async-done(((bf16[96,4608]{1,0:T(8,128)(2,1)}), bf16[3072,4608]{1,0:T(8,128)(2,1)}) %all-gather.2.cloned.1.call-update) | async-done | bytes 28311568 | tf_op jit(solution)/shard_map/all_gather | solution.py:60
  181.1 23.6 %fusion.33 = f32[640,4608]{1,0:T(8,128)S(1)} fusion(bf16[640,3072]{1,0:T(8,128)(2,1)} %fusion.25, bf16[3072,4608]{1,0:T(8,128)(2,1)} %all-gather.2.cloned.1.call-done), kind=kOutput, calls=%fused_computation.72 | convolution fusion | flops 18119393280 | bytes 44040192 | tf_op jit(solution)/shard_map/dot_general | solution.py:61
  204.7 5.2 slice_multiply_fusion
  210.1 5.5 copy.13
  215.6 2.3 reduce_sum.48
  218.1 4.1 mul.104
  222.2 5.5 mul.105
  227.8 4.3 multiply_convert_fusion
  234.6 4.3 collective-permute-start.1
  238.9 38.6 %collective-permute-done = bf16[2,1,1,2,2,80,1536]{6,5,4,3,1,2,0:T(8,128)(2,1)S(1)} collective-permute-done((bf16[2,1,1,2,2,80,1536]{6,5,4,3,1,2,0:T(8,128)(2,1)S(1)}, bf16[2,1,1,2,2,80,1536]{6,5,4,3,1,2,0:T(8,128)(2,1)S(1)}, u32[]{:S(2)}, u32[]{:S(2)}) %collective-permute-start) | collective-permute-done | bytes 1966112 | tf_op jit(solution)/shard_map/ppermute | solution.py:24
  281.3 3.4 fusion.32
  284.7 3.4 collective-permute-start.2
  290.7 5.5 copy.12
  296.1 2.6 multiply_reduce_fusion.1
  301.4 65.0 %collective-permute-done.2 = bf16[2,4,1,1,2,80,1536]{6,5,4,3,1,2,0:T(8,128)(2,1)} collective-permute-done((bf16[2,4,1,1,2,80,1536]{6,5,4,3,1,2,0:T(8,128)(2,1)}, bf16[2,4,1,1,2,80,1536]{6,5,4,3,1,2,0:T(8,128)(2,1)}, u32[]{:S(2)}, u32[]{:S(2)}) %collective-permute-start.2) | collective-permute-done | bytes 3932192 | tf_op jit(solution)/shard_map/ppermute | solution.py:24
  366.4 6.0 %collective-permute-done.3 = bf16[2,4,1,1,2,80,1536]{6,5,4,3,1,2,0:T(8,128)(2,1)} collective-permute-done((bf16[2,4,1,1,2,80,1536]{6,5,4,3,1,2,0:T(8,128)(2,1)}, bf16[2,4,1,1,2,80,1536]{6,5,4,3,1,2,0:T(8,128)(2,1)}, u32[]{:S(2)}, u32[]{:S(2)}) %collective-permute-start.3) | collective-permute-done | bytes 3932192 | tf_op jit(solution)/shard_map/ppermute | solution.py:26
  372.4 6.5 %pad_maximum_fusion = bf16[2,4,1,4,2,80,1536]{6,5,4,3,1,2,0:T(8,128)(2,1)S(1)} fusion(bf16[2,4,1,1,2,80,1536]{6,5,4,3,1,2,0:T(8,128)(2,1)} %collective-permute-done.3, bf16[2,1,1,2,2,80,1536]{6,5,4,3,1,2,0:T(8,128)(2,1)S(1)} %copy-done.8, bf16[1,2,1,2,2,80,1536]{6,5,4,3,1,2,0:T(8,128)(2,1)S(1)} %bitcast.72, ...), kind=kLoop, calls=%fused_computation.26 | loop fusion | flops 39321600 | bytes 31457280 | tf_op jit(solution)/shard_map/concatenate | solution.py:22
  378.8 5.8 fusion.31
  384.6 15.1 %squeeze.28 = bf16[2560,12,128]{2,1,0:T(8,128)(2,1)} reshape(bf16[1,4,1,4,2,80,1536]{6,5,4,3,1,2,0:T(8,128)(2,1)} %get-tuple-element.149) | data formatting | bytes 15728640 | tf_op jit(solution)/shard_map/squeeze | solution.py:73
  399.7 9.2 %copy.16 = bf16[12,2560,128]{2,1,0:T(8,128)(2,1)} copy(bf16[12,2560,128]{2,0,1:T(8,128)(2,1)} %bitcast.66) | data formatting | bytes 15728640
  408.9 15.1 %squeeze.29 = bf16[2560,12,128]{2,1,0:T(8,128)(2,1)} reshape(bf16[1,4,1,4,2,80,1536]{6,5,4,3,1,2,0:T(8,128)(2,1)} %get-tuple-element.148) | data formatting | bytes 15728640 | tf_op jit(solution)/shard_map/squeeze | solution.py:74
  424.0 9.3 %copy.17 = bf16[12,2560,128]{2,1,0:T(8,128)(2,1)} copy(bf16[12,2560,128]{2,0,1:T(8,128)(2,1)} %bitcast.67) | data formatting | bytes 15728640
  433.2 142.6 %while.11 = (s32[]{:T(128)}, bf16[12,640,128]{2,1,0:T(8,128)(2,1)S(1)}, pred[640]{0:T(1024)(128)(4,1)S(1)}, s32[12,3]{0,1:T(4,128)S(1)}, pred[1,2560]{1,0:T(4,12...) while((s32[]{:T(128)}, ...), condition=%wide.region_6.7_spmd.clone, body=%wide.region_4.6_spmd.clone.sunk | while | flops 866877440 | bytes 14808906 | solution.py:123
  433.9 8.9 %fusion.42 = (f32[640]{0:T(1024)S(1)}, f32[640,2560]{1,0:T(8,128)S(1)}) fusion(bf16[12,2560,128]{2,1,0:T(8,128)(2,1)} %get-tuple-element.290, s32[]{:T(128)} %get-tuple-element.268, bf16[12,640,128]{1,2,0:T(8,128)(2,1)} %get-tuple-element.289, pred[2560]{0:T(1024)(128)(4,1)S(1)} %reduce.4, s32[]{:T(128)} %bitcast.63, ...), kind=kOutput, calls=%fused_computation.69.clone.1 | convolution fusion | flops 444005760 | bytes 7418880 | tf_op jit(solution)/shard_map/while/body/eval_jaxpr/qd,kd->qk/dot_general | solution.py:114
  442.9 2.2 fusion.43
  445.8 8.9 %fusion.42 = (f32[640]{0:T(1024)S(1)}, f32[640,2560]{1,0:T(8,128)S(1)}) fusion(bf16[12,2560,128]{2,1,0:T(8,128)(2,1)} %get-tuple-element.290, s32[]{:T(128)} %get-tuple-element.268, bf16[12,640,128]{1,2,0:T(8,128)(2,1)} %get-tuple-element.289, pred[2560]{0:T(1024)(128)(4,1)S(1)} %reduce.4, s32[]{:T(128)} %bitcast.63, ...), kind=kOutput, calls=%fused_computation.69.clone.1 | convolution fusion | flops 444005760 | bytes 7418880 | tf_op jit(solution)/shard_map/while/body/eval_jaxpr/qd,kd->qk/dot_general | solution.py:114
  457.7 8.9 %fusion.42 = (f32[640]{0:T(1024)S(1)}, f32[640,2560]{1,0:T(8,128)S(1)}) fusion(bf16[12,2560,128]{2,1,0:T(8,128)(2,1)} %get-tuple-element.290, s32[]{:T(128)} %get-tuple-element.268, bf16[12,640,128]{1,2,0:T(8,128)(2,1)} %get-tuple-element.289, pred[2560]{0:T(1024)(128)(4,1)S(1)} %reduce.4, s32[]{:T(128)} %bitcast.63, ...), kind=kOutput, calls=%fused_computation.69.clone.1 | convolution fusion | flops 444005760 | bytes 7418880 | tf_op jit(solution)/shard_map/while/body/eval_jaxpr/qd,kd->qk/dot_general | solution.py:114
  466.6 2.2 fusion.43
  469.6 8.9 %fusion.42 = (f32[640]{0:T(1024)S(1)}, f32[640,2560]{1,0:T(8,128)S(1)}) fusion(bf16[12,2560,128]{2,1,0:T(8,128)(2,1)} %get-tuple-element.290, s32[]{:T(128)} %get-tuple-element.268, bf16[12,640,128]{1,2,0:T(8,128)(2,1)} %get-tuple-element.289, pred[2560]{0:T(1024)(128)(4,1)S(1)} %reduce.4, s32[]{:T(128)} %bitcast.63, ...), kind=kOutput, calls=%fused_computation.69.clone.1 | convolution fusion | flops 444005760 | bytes 7418880 | tf_op jit(solution)/shard_map/while/body/eval_jaxpr/qd,kd->qk/dot_general | solution.py:114
  478.5 2.2 fusion.43
  481.5 8.9 %fusion.42 = (f32[640]{0:T(1024)S(1)}, f32[640,2560]{1,0:T(8,128)S(1)}) fusion(bf16[12,2560,128]{2,1,0:T(8,128)(2,1)} %get-tuple-element.290, s32[]{:T(128)} %get-tuple-element.268, bf16[12,640,128]{1,2,0:T(8,128)(2,1)} %get-tuple-element.289, pred[2560]{0:T(1024)(128)(4,1)S(1)} %reduce.4, s32[]{:T(128)} %bitcast.63, ...), kind=kOutput, calls=%fused_computation.69.clone.1 | convolution fusion | flops 444005760 | bytes 7418880 | tf_op jit(solution)/shard_map/while/body/eval_jaxpr/qd,kd->qk/dot_general | solution.py:114
  493.4 8.9 %fusion.42 = (f32[640]{0:T(1024)S(1)}, f32[640,2560]{1,0:T(8,128)S(1)}) fusion(bf16[12,2560,128]{2,1,0:T(8,128)(2,1)} %get-tuple-element.290, s32[]{:T(128)} %get-tuple-element.268, bf16[12,640,128]{1,2,0:T(8,128)(2,1)} %get-tuple-element.289, pred[2560]{0:T(1024)(128)(4,1)S(1)} %reduce.4, s32[]{:T(128)} %bitcast.63, ...), kind=kOutput, calls=%fused_computation.69.clone.1 | convolution fusion | flops 444005760 | bytes 7418880 | tf_op jit(solution)/shard_map/while/body/eval_jaxpr/qd,kd->qk/dot_general | solution.py:114
  502.3 2.2 fusion.43
  505.2 8.9 %fusion.42 = (f32[640]{0:T(1024)S(1)}, f32[640,2560]{1,0:T(8,128)S(1)}) fusion(bf16[12,2560,128]{2,1,0:T(8,128)(2,1)} %get-tuple-element.290, s32[]{:T(128)} %get-tuple-element.268, bf16[12,640,128]{1,2,0:T(8,128)(2,1)} %get-tuple-element.289, pred[2560]{0:T(1024)(128)(4,1)S(1)} %reduce.4, s32[]{:T(128)} %bitcast.63, ...), kind=kOutput, calls=%fused_computation.69.clone.1 | convolution fusion | flops 444005760 | bytes 7418880 | tf_op jit(solution)/shard_map/while/body/eval_jaxpr/qd,kd->qk/dot_general | solution.py:114
  514.2 2.2 fusion.43
  517.1 8.9 %fusion.42 = (f32[640]{0:T(1024)S(1)}, f32[640,2560]{1,0:T(8,128)S(1)}) fusion(bf16[12,2560,128]{2,1,0:T(8,128)(2,1)} %get-tuple-element.290, s32[]{:T(128)} %get-tuple-element.268, bf16[12,640,128]{1,2,0:T(8,128)(2,1)} %get-tuple-element.289, pred[2560]{0:T(1024)(128)(4,1)S(1)} %reduce.4, s32[]{:T(128)} %bitcast.63, ...), kind=kOutput, calls=%fused_computation.69.clone.1 | convolution fusion | flops 444005760 | bytes 7418880 | tf_op jit(solution)/shard_map/while/body/eval_jaxpr/qd,kd->qk/dot_general | solution.py:114
  529.0 8.9 %fusion.42 = (f32[640]{0:T(1024)S(1)}, f32[640,2560]{1,0:T(8,128)S(1)}) fusion(bf16[12,2560,128]{2,1,0:T(8,128)(2,1)} %get-tuple-element.290, s32[]{:T(128)} %get-tuple-element.268, bf16[12,640,128]{1,2,0:T(8,128)(2,1)} %get-tuple-element.289, pred[2560]{0:T(1024)(128)(4,1)S(1)} %reduce.4, s32[]{:T(128)} %bitcast.63, ...), kind=kOutput, calls=%fused_computation.69.clone.1 | convolution fusion | flops 444005760 | bytes 7418880 | tf_op jit(solution)/shard_map/while/body/eval_jaxpr/qd,kd->qk/dot_general | solution.py:114
  537.9 2.2 fusion.43
  540.9 8.9 %fusion.42 = (f32[640]{0:T(1024)S(1)}, f32[640,2560]{1,0:T(8,128)S(1)}) fusion(bf16[12,2560,128]{2,1,0:T(8,128)(2,1)} %get-tuple-element.290, s32[]{:T(128)} %get-tuple-element.268, bf16[12,640,128]{1,2,0:T(8,128)(2,1)} %get-tuple-element.289, pred[2560]{0:T(1024)(128)(4,1)S(1)} %reduce.4, s32[]{:T(128)} %bitcast.63, ...), kind=kOutput, calls=%fused_computation.69.clone.1 | convolution fusion | flops 444005760 | bytes 7418880 | tf_op jit(solution)/shard_map/while/body/eval_jaxpr/qd,kd->qk/dot_general | solution.py:114
  549.8 2.2 fusion.43
  552.8 8.9 %fusion.42 = (f32[640]{0:T(1024)S(1)}, f32[640,2560]{1,0:T(8,128)S(1)}) fusion(bf16[12,2560,128]{2,1,0:T(8,128)(2,1)} %get-tuple-element.290, s32[]{:T(128)} %get-tuple-element.268, bf16[12,640,128]{1,2,0:T(8,128)(2,1)} %get-tuple-element.289, pred[2560]{0:T(1024)(128)(4,1)S(1)} %reduce.4, s32[]{:T(128)} %bitcast.63, ...), kind=kOutput, calls=%fused_computation.69.clone.1 | convolution fusion | flops 444005760 | bytes 7418880 | tf_op jit(solution)/shard_map/while/body/eval_jaxpr/qd,kd->qk/dot_general | solution.py:114
  564.7 8.9 %fusion.42 = (f32[640]{0:T(1024)S(1)}, f32[640,2560]{1,0:T(8,128)S(1)}) fusion(bf16[12,2560,128]{2,1,0:T(8,128)(2,1)} %get-tuple-element.290, s32[]{:T(128)} %get-tuple-element.268, bf16[12,640,128]{1,2,0:T(8,128)(2,1)} %get-tuple-element.289, pred[2560]{0:T(1024)(128)(4,1)S(1)} %reduce.4, s32[]{:T(128)} %bitcast.63, ...), kind=kOutput, calls=%fused_computation.69.clone.1 | convolution fusion | flops 444005760 | bytes 7418880 | tf_op jit(solution)/shard_map/while/body/eval_jaxpr/qd,kd->qk/dot_general | solution.py:114
  573.6 2.2 fusion.43
  577.1 2.9 copy.18
  580.0 2.6 reshape.192
  (124 shorter events, 31.3 us)
Async XLA Ops:
  6.5 7.0 %copy-start = (f32[128]{0:T(128)S(1)}, f32[128]{0:T(128)}, u32[]{:S(2)}) copy-start(f32[128]{0:T(128)} %param.15) | copy-start | bytes 1540
  6.5 174.6 %all-gather.2.cloned.1.call-start = ((), (), s32[]{:S(2)}) async-start(), calls=%async_computation | async-start | bytes 29196288 | tf_op jit(solution)/shard_map/all_gather | solution.py:60
  7.3 6.3 %copy-start.13 = (f32[3072]{0:T(1024)S(1)}, f32[3072]{0:T(1024)}, u32[]{:S(2)}) copy-start(f32[3072]{0:T(1024)} %param.11) | copy-start | bytes 36868
  7.3 6.3 %copy-start.14 = (f32[3072]{0:T(1024)S(1)}, f32[3072]{0:T(1024)}, u32[]{:S(2)}) copy-start(f32[3072]{0:T(1024)} %param.12) | copy-start | bytes 36868
  232.0 45.5 %copy-start.3 = (bf16[1,2,1,2,2,80,1536]{6,5,4,3,1,2,0:T(8,128)(2,1)}, bf16[1,2,1,2,2,80,1536]{6,5,4,3,1,2,0:T(8,128)(2,1)S(1)}, u32[]{:S(2)}) copy-start(bf16[1,2,1,2,2,80,1536]{6,5,4,3,1,2,0:T(8,128)(2,1)S(1)} %multiply_convert_fusion) | copy-start | bytes 5898244
  232.4 45.1 %collective-permute-start = (bf16[2,1,1,2,2,80,1536]{6,5,4,3,1,2,0:T(8,128)(2,1)S(1)}, bf16[2,1,1,2,2,80,1536]{6,5,4,3,1,2,0:T(8,128)(2,1)S(1)}, u32[]{:S(2)}, u32[]{:S(2)}) collective-permute-start(bf16[2,1,1,2,2,80,1536]{6,5,4,3,1,2,0:T(8,128)(2,1)S(1)} %get-tuple-element.155), channel_id=1, source_target_pairs={{0,4},{4,8},{8,12},{12,16},{16,20},{20,24},{24,28},{1,5},{5,9},{9,... | collective-permute-start | bytes 5898248 | tf_op jit(solution)/shard_map/ppermute | solution.py:24
  234.6 42.9 %collective-permute-start.1 = (bf16[2,1,1,2,2,80,1536]{6,5,4,3,1,2,0:T(8,128)(2,1)S(1)}, bf16[2,1,1,2,2,80,1536]{6,5,4,3,1,2,0:T(8,128)(2,1)S(1)}, u32[]{:S(2)}, u32[]{:S(2)}) collective-permute-start(bf16[2,1,1,2,2,80,1536]{6,5,4,3,1,2,0:T(8,128)(2,1)S(1)} %get-tuple-element.156), channel_id=1, source_target_pairs={{4,0},{8,4},{12,8},{16,12},{20,16},{24,20},{28,24},{5,1},{9,5},{13... | collective-permute-start | bytes 5898248 | tf_op jit(solution)/shard_map/ppermute | solution.py:26
  277.6 1.4 copy-start.5
  278.9 1.3 copy-start.7
  281.3 8.3 %copy-start.11 = (s32[16,16,80]{2,1,0:T(8,128)S(1)}, s32[16,16,80]{2,1,0:T(8,128)}, u32[]{:S(2)}) copy-start(s32[16,16,80]{2,1,0:T(8,128)} %param.17) | copy-start | bytes 245764
  284.7 81.7 %collective-permute-start.2 = (bf16[2,4,1,1,2,80,1536]{6,5,4,3,1,2,0:T(8,128)(2,1)}, bf16[2,4,1,1,2,80,1536]{6,5,4,3,1,2,0:T(8,128)(2,1)}, u32[]{:S(2)}, u32[]{:S(2)}) collective-permute-start(bf16[2,4,1,1,2,80,1536]{6,5,4,3,1,2,0:T(8,128)(2,1)} %get-tuple-element.153), channel_id=1, source_target_pairs={{0,1},{1,2},{2,3},{4,5},{5,6},{6,7},{8,9},{9,10},{10,11},{12,13},{... | collective-permute-start | bytes 11796488 | tf_op jit(solution)/shard_map/ppermute | solution.py:24
  288.1 84.3 %collective-permute-start.3 = (bf16[2,4,1,1,2,80,1536]{6,5,4,3,1,2,0:T(8,128)(2,1)}, bf16[2,4,1,1,2,80,1536]{6,5,4,3,1,2,0:T(8,128)(2,1)}, u32[]{:S(2)}, u32[]{:S(2)}) collective-permute-start(bf16[2,4,1,1,2,80,1536]{6,5,4,3,1,2,0:T(8,128)(2,1)} %get-tuple-element.154), channel_id=1, source_target_pairs={{1,0},{2,1},{3,2},{5,4},{6,5},{7,6},{9,8},{10,9},{11,10},{13,12},{... | collective-permute-start | bytes 11796488 | tf_op jit(solution)/shard_map/ppermute | solution.py:26
  296.1 3.3 copy-start.2
  296.1 3.3 copy-start.15
  298.7 73.6 %copy-start.4 = (bf16[1,2,1,2,2,80,1536]{6,5,4,3,1,2,0:T(8,128)(2,1)S(1)}, bf16[1,2,1,2,2,80,1536]{6,5,4,3,1,2,0:T(8,128)(2,1)}, u32[]{:S(2)}) copy-start(bf16[1,2,1,2,2,80,1536]{6,5,4,3,1,2,0:T(8,128)(2,1)} %copy-done.3) | copy-start | bytes 5898244
  298.7 73.6 %copy-start.6 = (bf16[2,1,1,2,2,80,1536]{6,5,4,3,1,2,0:T(8,128)(2,1)S(1)}, bf16[2,1,1,2,2,80,1536]{6,5,4,3,1,2,0:T(8,128)(2,1)}, u32[]{:S(2)}) copy-start(bf16[2,1,1,2,2,80,1536]{6,5,4,3,1,2,0:T(8,128)(2,1)} %copy-done.5) | copy-start | bytes 5898244
  298.7 73.6 %copy-start.8 = (bf16[2,1,1,2,2,80,1536]{6,5,4,3,1,2,0:T(8,128)(2,1)S(1)}, bf16[2,1,1,2,2,80,1536]{6,5,4,3,1,2,0:T(8,128)(2,1)}, u32[]{:S(2)}) copy-start(bf16[2,1,1,2,2,80,1536]{6,5,4,3,1,2,0:T(8,128)(2,1)} %copy-done.7) | copy-start | bytes 5898244
  424.0 9.3 %copy-start.9 = (bf16[12,640,128]{2,1,0:T(8,128)(2,1)S(1)}, bf16[12,640,128]{2,1,0:T(8,128)(2,1)}, u32[]{:S(2)}) copy-start(bf16[12,640,128]{2,1,0:T(8,128)(2,1)} %custom-call) | copy-start | bytes 5898244
  424.0 9.3 %copy-start.12 = (s32[12,3]{0,1:T(4,128)S(1)}, s32[12,3]{0,1:T(4,128)}, u32[]{:S(2)}) copy-start(s32[12,3]{0,1:T(4,128)} %param.16) | copy-start | bytes 436
  575.8 1.3 copy-start.10
  577.1 5.5 copy-start.1
Sparse Core Ops, SparseCore 0:
  10.2 170.8 all-gather.1
where the time goes:
time: 597 us; the launch traced here: 589 us
  waiting for transfers between devices  273 us (46%)
  matrix products  157 us (26%)
  local copies, waits for them, and re-layouts  97.9 us (16%)
  other arithmetic  35.9 us (6%)
  between operations  13.7 us (2%)
  starting transfers between devices  11.3 us (2%)
    all_gather x1, waiting for transfers between devices, per_device(): full_weight = lax.all_gather(w_qkv, ('tm', 'height'), axis=0, tiled=True)  163 us
    dot_general x12, matrix products, per_head(): jnp.einsum('qd,kd->qk', query_one, key_one, preferred_element_type=jnp.fl...  107 us
    ppermute x2, waiting for transfers between devices, with_halo(): lax.ppermute(tail, axis, [(i, (i + 1) % count) for i in range(ends)])  104 us
    dot_general x12, matrix products, per_head(): result = jnp.dot(weights, value_one, preferred_element_type=jnp.float32)  26.6 us
    dot_general x1, matrix products, per_device(): qkv = jnp.dot(modulated, full_weight, preferred_element_type=jnp.float32)  23.6 us
    unnamed x34, local copies, waits for them, and re-layouts  23.1 us
    squeeze x1, local copies, waits for them, and re-layouts, per_device(): key_heads = jnp.transpose(extended[0], (1, 0, 2))  15.1 us
    squeeze x1, local copies, waits for them, and re-layouts, per_device(): value_heads = jnp.transpose(extended[1], (1, 0, 2))  15.1 us
  transfers between devices with their start and end apart: 5, of which 4 were waited for; matrix products, arithmetic and copies ran while one was open for 4% of the time, Pallas kernels for 0%

commit v1 on v0

v1 whole, which is shorter than its diff:
```python
import functools

import jax
import jax.numpy as jnp
import numpy as np
from jax import lax
from jax.experimental import pallas as pl
from jax.experimental.pallas import tpu as pltpu
from jax.sharding import Mesh
from jax.sharding import PartitionSpec as P

HDIM = 128
HEADS = 12
TT = 1
TH = 2
TW = 8
CORES = 2
GROUP = 6
EPS = 1e-06
VMEM = 56 * 1024 * 1024


def modulate(tokens, mod_scale, mod_shift):
    values = tokens.astype(jnp.float32)
    mean = jnp.mean(values, axis=-1, keepdims=True)
    centred = values - mean
    variance = jnp.mean(centred * centred, axis=-1, keepdims=True)
    normed = centred * lax.rsqrt(variance + EPS)
    return (normed * (1.0 + mod_scale) + mod_shift).astype(jnp.bfloat16)


def gather_columns(w_qkv, spans):
    part = jnp.concatenate([w_qkv[:, start:stop] for start, stop in spans], axis=1)
    own = lax.all_gather(part, ("chip", "height"), axis=0, tiled=True)
    other = lax.ppermute(own, "core", [(i, CORES - 1 - i) for i in range(CORES)])
    return own, other


def project_body(x_own, x_other, w_own, w_other, gain, out, *, normed):
    total = jnp.dot(x_own[...], w_own[...], preferred_element_type=jnp.float32)
    total += jnp.dot(x_other[...], w_other[...], preferred_element_type=jnp.float32)

    def plain():
        out[0] = total.astype(out.dtype)

    def norm():
        for start in range(0, total.shape[1], HDIM):
            head = total[:, start : start + HDIM]
            power = jnp.mean(head * head, axis=-1, keepdims=True)
            out[0, :, start : start + HDIM] = (head * lax.rsqrt(power + EPS) * gain[...]).astype(out.dtype)

    step = pl.program_id(0)
    if normed is None:
        norm()
    else:
        pl.when(step < normed)(norm)
        pl.when(step >= normed)(plain)


def project(x_own, x_other, w_own, w_other, gain, parts, normed_parts):
    rows, depth = x_own.shape
    columns = w_own.shape[1]
    block = 2 * HDIM
    per_part = columns // parts // block
    steps = columns // block
    normed = None if normed_parts == parts else normed_parts * per_part
    whole = lambda j: (0, 0)
    slab = lambda j: (0, j)
    return pl.pallas_call(
        functools.partial(project_body, normed=normed),
        grid=(steps,),
        in_specs=[
            pl.BlockSpec((rows, depth), whole),
            pl.BlockSpec((rows, depth), whole),
            pl.BlockSpec((depth, block), slab),
            pl.BlockSpec((depth, block), slab),
            pl.BlockSpec((1, HDIM), whole),
        ],
        out_specs=pl.BlockSpec((1, rows, block), lambda j: (j // per_part, 0, j % per_part)),
        out_shape=jax.ShapeDtypeStruct((parts, rows, columns // parts), jnp.bfloat16),
        compiler_params=pltpu.CompilerParams(vmem_limit_bytes=VMEM),
        cost_estimate=pl.CostEstimate(
            flops=4 * rows * depth * columns,
            bytes_accessed=4 * depth * columns + 4 * rows * depth + 2 * rows * columns,
            transcendentals=0,
        ),
    )(x_own, x_other, w_own, w_other, gain.reshape(1, HDIM))


def attend_body(window, query, own, above, below, before, after, valid, *rest, frames, tiles, cell, first):
    out, keys, values, band = rest[-4:]
    group = pl.program_id(0)
    head = first + group
    width = cell // TH
    inner = tiles * cell

    @pl.when(group == 0)
    def _():
        values[:, :, HDIM:] = valid[...]
        q_tile = lax.broadcasted_iota(jnp.int32, (cell, 3 * cell), 0)
        k_tile = lax.broadcasted_iota(jnp.int32, (cell, 3 * cell), 1)
        apart = jnp.abs(lax.rem(q_tile, width) // TW - lax.rem(k_tile, width) // TW)
        for reach in range(3):
            band[reach] = jnp.where(apart <= reach, 1.0, 0.0).astype(band.dtype)

    for which, store in ((0, keys), (1, values)):
        def put(frame, rows, block):
            if which:
                block = block * valid[frame, rows, :]
            store[frame, rows, :HDIM] = block

        for frame in range(frames):
            put(frame + 1, pl.ds(0, cell), above[which, frame])
            put(frame + 1, pl.ds(cell, inner), own[which, frame])
            put(frame + 1, pl.ds(cell + inner, cell), below[which, frame])
        put(0, pl.ds(0, inner + 2 * cell), before[which])
        put(frames + 1, pl.ds(0, inner + 2 * cell), after[which])

    scale = np.float32(np.log2(np.e) / np.sqrt(HDIM))
    reach_t, reach_h, reach_w = window[head, 0], window[head, 1], window[head, 2]

    def attend(over_t, over_h):
        seen = (3 if over_h else 1) * cell
        mask = band[reach_w, :, :seen]
        for frame in range(frames):
            for tile in range(tiles):
                start = (frame * tiles + tile) * cell
                rows = pl.ds((tile + (0 if over_h else 1)) * cell, seen)
                mine = query[pl.ds(start, cell), :]
                total = None
                for step in (-1, 0, 1) if over_t else (0,):
                    source = frame + 1 + step
                    scores = lax.dot_general(
                        mine,
                        keys[source, rows, :],
                        (((1,), (1,)), ((), ())),
                        preferred_element_type=jnp.float32,
                    )
                    terms = jnp.exp2(scores * scale).astype(jnp.bfloat16) * mask
                    part = jnp.dot(terms, values[source, rows, :], preferred_element_type=jnp.float32)
                    total = part if total is None else total + part
                here = valid[frame + 1, pl.ds((tile + 1) * cell, cell), :] > 0
                weight = jnp.where(here, total[:, HDIM:], 1.0)
                result = jnp.where(here, total[:, :HDIM] / weight, 0.0)
                out[pl.ds(start, cell), :] = result.astype(out.dtype)

    for over_t in (False, True):
        for over_h in (False, True):
            pl.when(((reach_t > 0) == over_t) & ((reach_h > 0) == over_h))(
                functools.partial(attend, over_t, over_h)
            )


def attend(window, query, own, above, below, before, after, valid, first, total_heads, onto=None):
    _, frames, inner, columns = own.shape
    heads = columns // HDIM
    cell = above.shape[2]
    tiles = inner // cell
    rows = query.shape[0]
    span = inner + 2 * cell
    specs = [
        pl.BlockSpec((rows, HDIM), lambda h, w: (0, h)),
        pl.BlockSpec((2, frames, inner, HDIM), lambda h, w: (0, 0, 0, h)),
        pl.BlockSpec((2, frames, cell, HDIM), lambda h, w: (0, 0, 0, h)),
        pl.BlockSpec((2, frames, cell, HDIM), lambda h, w: (0, 0, 0, h)),
        pl.BlockSpec((2, span, HDIM), lambda h, w: (0, 0, h)),
        pl.BlockSpec((2, span, HDIM), lambda h, w: (0, 0, h)),
        pl.BlockSpec((frames + 2, span, HDIM), lambda h, w: (0, 0, 0)),
    ]
    operands = [window, query, own, above, below, before, after, valid]
    aliases = {}
    if onto is not None:
        specs.append(pl.BlockSpec(memory_space=pl.ANY))
        operands.append(onto)
        aliases = {len(operands) - 1: 0}
    return pl.pallas_call(
        functools.partial(attend_body, frames=frames, tiles=tiles, cell=cell, first=first),
        grid_spec=pltpu.PrefetchScalarGridSpec(
            num_scalar_prefetch=1,
            grid=(heads,),
            in_specs=specs,
            out_specs=pl.BlockSpec((rows, HDIM), lambda h, w: (0, first + h)),
            scratch_shapes=[
                pltpu.VMEM((frames + 2, span, HDIM), jnp.bfloat16),
                pltpu.VMEM((frames + 2, span, 2 * HDIM), jnp.bfloat16),
                pltpu.VMEM((3, cell, 3 * cell), jnp.bfloat16),
            ],
        ),
        out_shape=jax.ShapeDtypeStruct((rows, total_heads * HDIM), jnp.bfloat16),
        input_output_aliases=aliases,
        compiler_params=pltpu.CompilerParams(vmem_limit_bytes=VMEM),
        cost_estimate=pl.CostEstimate(
            flops=heads * rows * 9 * cell * HDIM * 6,
            bytes_accessed=2 * columns * (2 * rows + 2 * (frames + 2) * span),
            transcendentals=heads * rows * 9 * cell,
        ),
    )(*operands)


def halo(kv, frames, rows, width):
    parts, _, columns = kv.shape
    cell = TH * width
    grid = kv.reshape(parts, frames, rows * width, columns)
    up = lax.axis_size("height")
    above = lax.ppermute(grid[:, :, rows * width - cell :], "height", [(i, i + 1) for i in range(up - 1)])
    below = lax.ppermute(grid[:, :, :cell], "height", [(i + 1, i) for i in range(up - 1)])
    along = ("chip", "core")
    count = lax.axis_size("chip") * lax.axis_size("core")
    last = jnp.concatenate([above[:, -1], grid[:, -1], below[:, -1]], axis=1)
    head = jnp.concatenate([above[:, 0], grid[:, 0], below[:, 0]], axis=1)
    before = lax.ppermute(last, along, [(i, i + 1) for i in range(count - 1)])
    after = lax.ppermute(head, along, [(i + 1, i) for i in range(count - 1)])
    return grid, above, below, before, after


def per_device(tokens, mod_scale, mod_shift, w_qkv, q_gain, k_gain, window, valid):
    frames, rows, width, features = tokens.shape
    count = frames * rows * width
    inner = w_qkv.shape[1] // 3
    chips = lax.axis_size("chip")
    core = lax.axis_index("core")

    step = GROUP * HDIM
    starts = range(0, inner, step)
    kv_weights = [
        gather_columns(w_qkv, [(inner + s, inner + s + step), (2 * inner + s, 2 * inner + s + step)])
        for s in starts
    ]
    q_weights = [gather_columns(w_qkv, [(s, s + step)]) for s in starts]

    modulated = modulate(tokens.reshape(count, features), mod_scale, mod_shift)
    slabs = modulated.reshape(count, chips, CORES, features // chips // CORES)
    x_own = lax.dynamic_index_in_dim(slabs, core, 2, False).reshape(count, features // CORES)
    x_other = lax.dynamic_index_in_dim(slabs, CORES - 1 - core, 2, False).reshape(count, features // CORES)

    valid_pad = jnp.pad(valid, ((TT, TT), (TH, TH), (0, 0)))
    first_frame = (lax.axis_index("chip") * CORES + core) * frames
    first_row = lax.axis_index("height") * rows
    near = lax.dynamic_slice(
        valid_pad, (first_frame, first_row, jnp.int32(0)), (frames + 2 * TT, rows + 2 * TH, width)
    )
    near = jnp.broadcast_to(
        (near > 0).astype(jnp.bfloat16).reshape(frames + 2 * TT, -1, 1),
        (frames + 2 * TT, (rows + 2 * TH) * width, HDIM),
    )

    cells = [
        halo(project(x_own, x_other, own, other, k_gain, 2, 1), frames, rows, width)
        for own, other in kv_weights
    ]
    queries = [project(x_own, x_other, own, other, q_gain, 1, 1)[0] for own, other in q_weights]
    out = None
    for index, (query, parts) in enumerate(zip(queries, cells)):
        out = attend(window, query, *parts, near, index * GROUP, HEADS, out)
    return out.reshape(frames, rows, width, inner)


def solution(mesh):
    split = Mesh(
        mesh.devices.reshape(mesh.shape["tm"] // CORES, CORES, mesh.shape["height"]),
        ("chip", "core", "height"),
    )
    in_specs = (
        P(("chip", "core"), "height", None, None),
        P(),
        P(),
        P(("chip", "core", "height"), None),
        P(),
        P(),
        P(),
        P(),
    )
    out_specs = P(("chip", "core"), "height", None, None)
    return jax.shard_map(
        per_device, mesh=split, in_specs=in_specs, out_specs=out_specs, check_vma=False
    )
```

time: 597 us -> 457 us (0.77); the launches traced: 589 us -> 456 us
  matrix products: 157 us -> 0 us
  local copies, waits for them, and re-layouts: 97.9 us -> 29.6 us
  Pallas kernels: 0 us -> 65.3 us
  waiting for transfers between devices: 273 us -> 306 us
  other arithmetic: 35.9 us -> 22.2 us
  starting transfers between devices: 11.3 us -> 19.8 us
    dot_general x25 -> x0, matrix products: 157 us -> none  [the longest x12 107 us: per_head(): jnp.einsum('qd,kd->qk', query_one, key_one, preferred_element_type=jnp.fl...]
    all_gather x1 -> x4, waiting for transfers between devices: 163 us -> 260 us  [gather_columns(): own = lax.all_gather(part, ('chip', 'height'), axis=0, tiled=True)]
    pallas_call x0 -> x6, Pallas kernels: none -> 65.3 us  [the longest x4 39.1 us: project(): pl.pallas_call(functools.partial(project_body, normed=normed), grid=(step...]
    ppermute x4 -> x12, waiting for transfers between devices: 110 us -> 45.2 us  [the longest x2 27.1 us: halo(): before = lax.ppermute(last, along, [(i, i + 1) for i in range(count - 1)])]
    squeeze x2 -> x6, local copies, waits for them, and re-layouts: 30.2 us -> 0.52 us  [halo(): head = jnp.concatenate([above[:, 0], grid[:, 0], below[:, 0]], axis=1)]
    unnamed x34 -> x27, local copies, waits for them, and re-layouts: 23.1 us -> 6.08 us
    slice x16 -> x3, local copies, waits for them, and re-layouts: 21.9 us -> 5.43 us  [the longest x2 3.39 us: halo(): grid[:, :, :cell]]
    mul x4 -> x2, local copies, waits for them, and re-layouts: 15.1 us -> 0.02 us  [modulate(): return (normed * (1.0 + mod_scale) + mod_shift).astype(jnp.bfloat16)]
  transfers between devices with their start and end apart: 5 -> 16, of which waited for: 4 -> 10; matrix products, arithmetic and copies ran while one was open for 4% -> 11% of each run, Pallas kernels for 0% -> 12%
where the time goes in v1:
time: 457 us; the launch traced here: 456 us
  waiting for transfers between devices  306 us (67%)
  Pallas kernels  65.3 us (14%)
  local copies, waits for them, and re-layouts  29.6 us (6%)
  other arithmetic  22.2 us (5%)
  starting transfers between devices  19.8 us (4%)
  between operations  13.4 us (3%)
    all_gather x4, waiting for transfers between devices, gather_columns(): own = lax.all_gather(part, ('chip', 'height'), axis=0, tiled=True)  260 us
    pallas_call x4, Pallas kernels, project(): pl.pallas_call(functools.partial(project_body, normed=normed), grid=(step...  39.1 us
    ppermute x2, waiting for transfers between devices, halo(): before = lax.ppermute(last, along, [(i, i + 1) for i in range(count - 1)])  27.1 us
    pallas_call x2, Pallas kernels, attend(): pl.pallas_call(functools.partial(attend_body, frames=frames, tiles=tiles,...  26.2 us
    ppermute x2, waiting for transfers between devices, halo(): lax.ppermute(grid[:, :, rows * width - cell:], 'height', [(i, i + 1) for...  11.6 us
    convert_element_type x1, local copies, waits for them, and re-layouts, modulate(): values = tokens.astype(jnp.float32)  10.6 us
  transfers between devices with their start and end apart: 16, of which 10 were waited for; matrix products, arithmetic and copies ran while one was open for 11% of the time, Pallas kernels for 12%

profile of v1, /device:TPU:4, one launch (start us, length us, event | category | flops | bytes accessed | tf_op | source)
XLA Modules:
  0.0 456.1 jit_solution(16217682382885341519)
XLA Ops:
  6.5 2.0 fusion.8
  8.6 0.7 pad_maximum_fusion.5
  9.4 0.7 pad_maximum_fusion.4
  10.9 80.9 %all-gather.11.cloned.1.call-done.w_own = bf16[1536,1536]{1,0:T(8,128)(2,1)} async-done(((bf16[96,1536]{1,0:T(8,128)(2,1)}), bf16[1536,1536]{1,0:T(8,128)(2,1)}) %all-gather.11.cloned.1.call-update) | async-done | bytes 4718608 | tf_op jit(solution)/shard_map/all_gather | solution.py:34
  91.8 81.8 %all-gather.7.cloned.1.call-done.w_own = bf16[1536,1536]{1,0:T(8,128)(2,1)} async-done(((bf16[96,1536]{1,0:T(8,128)(2,1)}), bf16[1536,1536]{1,0:T(8,128)(2,1)}) %all-gather.7.cloned.1.call-update) | async-done | bytes 4718608 | tf_op jit(solution)/shard_map/all_gather | solution.py:34
  173.6 10.6 %reshape.93 = f32[640,4,2,384]{3,2,1,0:T(2,128)} reshape(bf16[2,4,80,3072]{3,2,1,0:T(8,128)(2,1)} %param.8) | data formatting | bytes 11796480 | tf_op jit(solution)/shard_map/convert_element_type | solution.py:24
  184.3 2.8 convert_reduce_fusion
  187.1 3.3 multiply_reduce_fusion
  190.6 8.9 %fusion.3 = bf16[640,4,2,384]{3,1,0,2:T(4,128)(2,1)S(1)} fusion(f32[640,4,2,384]{3,2,1,0:T(2,128)} %reshape.93, f32[4,2,384]{2,0,1:T(4,128)S(1)} %copy.21, f32[4,2,384]{2,0,1:T(4,128)S(1)} %copy.20, f32[640]{0:T(1024)S(1)} %rsqrt.12, f32[640]{0:T(1024)S(1)} %div.9), kind=kLoop, calls=%fused_computation.4 | loop fusion | flops 9830400 | bytes 11826176 | tf_op jit(solution)/shard_map/convert_element_type | solution.py:29
  199.5 1.4 constant_dynamic-slice_fusion
  200.9 1.6 copy.44
  202.5 1.6 copy.45
  204.1 33.3 %all-gather.9.cloned.1.call-done.w_own = bf16[1536,768]{1,0:T(8,128)(2,1)} async-done(((bf16[96,768]{1,0:T(8,128)(2,1)}), bf16[1536,768]{1,0:T(8,128)(2,1)}) %all-gather.9.cloned.1.call-update) | async-done | bytes 2359312 | tf_op jit(solution)/shard_map/all_gather | solution.py:34
  237.4 63.7 %all-gather.5.cloned.1.call-done.w_own = bf16[1536,768]{1,0:T(8,128)(2,1)} async-done(((bf16[96,768]{1,0:T(8,128)(2,1)}), bf16[1536,768]{1,0:T(8,128)(2,1)}) %all-gather.5.cloned.1.call-update) | async-done | bytes 2359312 | tf_op jit(solution)/shard_map/all_gather | solution.py:34
  301.1 12.0 %shard_map.85 = bf16[2,640,768]{2,1,0:T(8,128)(2,1)} custom-call(bf16[640,1536]{1,0:T(8,128)(2,1)} %bitcast.57, bf16[640,1536]{1,0:T(8,128)(2,1)} %bitcast.61, bf16[1536,1536]{1,0:T(8,128)(2,1)} %all-gather.11.cloned.1.call-done.w_own, bf16[1536,1536]{1,0:T(8,128)(2,1)} %collective-permute-done.7.w_other, f32[1,128]{1,0:T(1,128)} %bitcast.65), custom_call_target="tpu_custom_call" | custom-call | flops 6039797760 | bytes 15335424 | tf_op jit(solution)/shard_map/pallas_call | solution.py:69
  313.1 1.6 fusion.6
  314.7 1.0 copy.40
  315.7 3.8 collective-permute-start.8
  319.6 1.0 copy.41
  320.6 1.3 collective-permute-start.9
  321.9 12.0 %shard_map.83 = bf16[2,640,768]{2,1,0:T(8,128)(2,1)} custom-call(bf16[640,1536]{1,0:T(8,128)(2,1)} %bitcast.58, bf16[640,1536]{1,0:T(8,128)(2,1)} %bitcast.62, bf16[1536,1536]{1,0:T(8,128)(2,1)} %all-gather.7.cloned.1.call-done.w_own, bf16[1536,1536]{1,0:T(8,128)(2,1)} %collective-permute-done.1.w_other, f32[1,128]{1,0:T(1,128)} %bitcast.66), custom_call_target="tpu_custom_call" | custom-call | flops 6039797760 | bytes 15335424 | tf_op jit(solution)/shard_map/pallas_call | solution.py:69
  333.9 1.8 fusion.7
  335.8 4.7 %collective-permute-start.2 = (bf16[2,2,160,768]{3,2,0,1:T(8,128)(2,1)S(1)}, bf16[2,2,160,768]{3,2,0,1:T(8,128)(2,1)S(1)}, u32[]{:S(2)}, u32[]{:S(2)}) collective-permute-start(bf16[2,2,160,768]{3,2,0,1:T(8,128)(2,1)S(1)} %copy.36), channel_id=1, source_target_pairs={{0,1},{1,2},{2,3},{4,5},{5,6},{6,7},{8,9},{9,10},{10,11},{12,13},{... | collective-permute-start | bytes 2949128 | tf_op jit(solution)/shard_map/ppermute | solution.py:205
  340.9 1.0 collective-permute-done.8
  341.9 1.5 collective-permute-start.3
  343.4 3.3 collective-permute-done.9
  346.8 1.5 pad_maximum_fusion.3
  348.3 2.1 collective-permute-start.11
  350.5 1.4 pad_maximum_fusion.2
  351.9 10.6 %collective-permute-done.2 = bf16[2,2,160,768]{3,2,0,1:T(8,128)(2,1)S(1)} collective-permute-done((bf16[2,2,160,768]{3,2,0,1:T(8,128)(2,1)S(1)}, bf16[2,2,160,768]{3,2,0,1:T(8,128)(2,1)S(1)}, u32[]{:S(2)}, u32[]{:S(2)}) %collective-permute-start.2) | collective-permute-done | bytes 983072 | tf_op jit(solution)/shard_map/ppermute | solution.py:205
  362.5 1.9 collective-permute-start.10
  364.4 3.2 collective-permute-done.3
  367.7 1.4 pad_maximum_fusion.1
  369.2 1.9 collective-permute-start.5
  371.1 1.4 pad_maximum_fusion
  372.5 2.4 collective-permute-start.4
  375.1 0.7 copy.33.window
  375.7 7.5 %shard_map.84 = bf16[1,640,768]{2,1,0:T(8,128)(2,1)} custom-call(bf16[640,1536]{1,0:T(8,128)(2,1)} %bitcast.59, bf16[640,1536]{1,0:T(8,128)(2,1)} %bitcast.63, bf16[1536,768]{1,0:T(8,128)(2,1)} %all-gather.9.cloned.1.call-done.w_own, bf16[1536,768]{1,0:T(8,128)(2,1)} %collective-permute-done.6.w_other, f32[1,128]{1,0:T(1,128)} %bitcast.67), custom_call_target="tpu_custom_call" | custom-call | flops 3019898880 | bytes 9633792 | tf_op jit(solution)/shard_map/pallas_call | solution.py:69
  383.2 7.6 %shard_map.82 = bf16[1,640,768]{2,1,0:T(8,128)(2,1)} custom-call(bf16[640,1536]{1,0:T(8,128)(2,1)} %bitcast.60, bf16[640,1536]{1,0:T(8,128)(2,1)} %bitcast.64, bf16[1536,768]{1,0:T(8,128)(2,1)} %all-gather.5.cloned.1.call-done.w_own, bf16[1536,768]{1,0:T(8,128)(2,1)} %collective-permute-done.w_other, f32[1,128]{1,0:T(1,128)} %bitcast.68), custom_call_target="tpu_custom_call" | custom-call | flops 3019898880 | bytes 9633792 | tf_op jit(solution)/shard_map/pallas_call | solution.py:69
  390.9 1.0 copy.31.above
  391.9 1.0 copy.32.below
  392.9 1.0 copy.34.above
  393.9 1.0 copy.35.below
  395.0 15.8 %collective-permute-done.10.before = bf16[2,640,768]{2,1,0:T(8,128)(2,1)} collective-permute-done((bf16[2,640,768]{2,1,0:T(8,128)(2,1)}, bf16[2,640,768]{2,1,0:T(8,128)(2,1)}, u32[]{:S(2)}, u32[]{:S(2)}) %collective-permute-start.10) | collective-permute-done | bytes 1966112 | tf_op jit(solution)/shard_map/ppermute | solution.py:211
  410.7 1.2 broadcast_in_dim.16.valid
  412.0 14.5 %shard_map.86.rest_0_ = bf16[640,1536]{1,0:T(8,128)(2,1)} custom-call(s32[12,3]{1,0:T(8,128)} %copy.33.window, bf16[640,768]{1,0:T(8,128)(2,1)} %bitcast.70, bf16[2,2,320,768]{3,2,1,0:T(8,128)(2,1)} %bitcast.50, bf16[2,2,160,768]{3,2,1,0:T(8,128)(2,1)} %copy.31.above, bf16[2,2,160,768]{3,2,1,0:T(8,128)(2,1)} %copy.32.below, ...), custom_call_target="tpu_custom_call" | custom-call | flops 4246732800 | bytes 9830400 | tf_op jit(solution)/shard_map/pallas_call | solution.py:176
  426.5 11.3 %collective-permute-done.4.before = bf16[2,640,768]{2,1,0:T(8,128)(2,1)} collective-permute-done((bf16[2,640,768]{2,1,0:T(8,128)(2,1)}, bf16[2,640,768]{2,1,0:T(8,128)(2,1)}, u32[]{:S(2)}, u32[]{:S(2)}) %collective-permute-start.4) | collective-permute-done | bytes 1966112 | tf_op jit(solution)/shard_map/ppermute | solution.py:211
  437.8 11.8 %shard_map.87 = bf16[640,1536]{1,0:T(8,128)(2,1)} custom-call(s32[12,3]{1,0:T(8,128)} %copy.33.window, bf16[640,768]{1,0:T(8,128)(2,1)} %bitcast.69, bf16[2,2,320,768]{3,2,1,0:T(8,128)(2,1)} %bitcast.53, bf16[2,2,160,768]{3,2,1,0:T(8,128)(2,1)} %copy.34.above, bf16[2,2,160,768]{3,2,1,0:T(8,128)(2,1)} %copy.35.below, ...), custom_call_target="tpu_custom_call", output_to_operand_aliasing={{}: (8, {})} | custom-call | flops 4246732800 | bytes 9830400 | tf_op jit(solution)/shard_map/pallas_call | solution.py:176
  (57 shorter events, 1.9 us)
Async XLA Ops:
  6.5 85.3 %all-gather.11.cloned.1.call-start = ((), (), s32[]{:S(2)}) async-start(), calls=%async_computation.3 | async-start | bytes 5013504 | tf_op jit(solution)/shard_map/all_gather | solution.py:34
  9.3 164.3 %all-gather.7.cloned.1.call-start = ((), (), s32[]{:S(2)}) async-start(), calls=%async_computation.1 | async-start | bytes 5013504 | tf_op jit(solution)/shard_map/all_gather | solution.py:34
  10.1 227.2 %all-gather.9.cloned.1.call-start = ((), (), s32[]{:S(2)}) async-start(), calls=%async_computation.2 | async-start | bytes 2506752 | tf_op jit(solution)/shard_map/all_gather | solution.py:34
  10.9 290.2 %all-gather.5.cloned.1.call-start = ((), (), s32[]{:S(2)}) async-start(), calls=%async_computation | async-start | bytes 2506752 | tf_op jit(solution)/shard_map/all_gather | solution.py:34
  91.8 209.3 %collective-permute-start.7 = (bf16[1536,1536]{1,0:T(8,128)(2,1)}, bf16[1536,1536]{1,0:T(8,128)(2,1)}, u32[]{:S(2)}, u32[]{:S(2)}) collective-permute-start(bf16[1536,1536]{1,0:T(8,128)(2,1)} %all-gather.11.cloned.1.call-done.w_own), channel_id=1, source_target_pairs={{0,4},{4,0},{1,5},{5,1},{2,6},{6,2},{3,7},{7,3},{8,12},{12,8},{9,1... | collective-permute-start | bytes 14155784 | tf_op jit(solution)/shard_map/ppermute | solution.py:35
  173.6 148.3 %collective-permute-start.1 = (bf16[1536,1536]{1,0:T(8,128)(2,1)}, bf16[1536,1536]{1,0:T(8,128)(2,1)}, u32[]{:S(2)}, u32[]{:S(2)}) collective-permute-start(bf16[1536,1536]{1,0:T(8,128)(2,1)} %all-gather.7.cloned.1.call-done.w_own), channel_id=1, source_target_pairs={{0,4},{4,0},{1,5},{5,1},{2,6},{6,2},{3,7},{7,3},{8,12},{12,8},{9,1... | collective-permute-start | bytes 14155784 | tf_op jit(solution)/shard_map/ppermute | solution.py:35
  184.2 6.3 %copy-start.7 = (f32[3072]{0:T(1024)S(1)}, f32[3072]{0:T(1024)}, u32[]{:S(2)}) copy-start(f32[3072]{0:T(1024)} %param.9) | copy-start | bytes 36868
  184.3 6.3 %copy-start.8 = (f32[3072]{0:T(1024)S(1)}, f32[3072]{0:T(1024)}, u32[]{:S(2)}) copy-start(f32[3072]{0:T(1024)} %param.10) | copy-start | bytes 36868
  237.4 135.1 %collective-permute-start.6 = (bf16[1536,768]{1,0:T(8,128)(2,1)}, bf16[1536,768]{1,0:T(8,128)(2,1)}, u32[]{:S(2)}, u32[]{:S(2)}) collective-permute-start(bf16[1536,768]{1,0:T(8,128)(2,1)} %all-gather.9.cloned.1.call-done.w_own), channel_id=1, source_target_pairs={{0,4},{4,0},{1,5},{5,1},{2,6},{6,2},{3,7},{7,3},{8,12},{12,8},{9,1... | collective-permute-start | bytes 7077896 | tf_op jit(solution)/shard_map/ppermute | solution.py:35
  301.1 82.1 %collective-permute-start = (bf16[1536,768]{1,0:T(8,128)(2,1)}, bf16[1536,768]{1,0:T(8,128)(2,1)}, u32[]{:S(2)}, u32[]{:S(2)}) collective-permute-start(bf16[1536,768]{1,0:T(8,128)(2,1)} %all-gather.5.cloned.1.call-done.w_own), channel_id=1, source_target_pairs={{0,4},{4,0},{1,5},{5,1},{2,6},{6,2},{3,7},{7,3},{8,12},{12,8},{9,1... | collective-permute-start | bytes 7077896 | tf_op jit(solution)/shard_map/ppermute | solution.py:35
  315.7 26.2 %collective-permute-start.8 = (bf16[2,2,160,768]{3,2,0,1:T(8,128)(2,1)}, bf16[2,2,160,768]{3,2,0,1:T(8,128)(2,1)S(1)}, u32[]{:S(2)}, u32[]{:S(2)}) collective-permute-start(bf16[2,2,160,768]{3,2,0,1:T(8,128)(2,1)} %copy.40), channel_id=1, source_target_pairs={{0,1},{1,2},{2,3},{4,5},{5,6},{6,7},{8,9},{9,10},{10,11},{12,13},{... | collective-permute-start | bytes 2949128 | tf_op jit(solution)/shard_map/ppermute | solution.py:205
  320.6 26.2 %collective-permute-start.9 = (bf16[2,2,160,768]{3,2,0,1:T(8,128)(2,1)}, bf16[2,2,160,768]{3,2,0,1:T(8,128)(2,1)S(1)}, u32[]{:S(2)}, u32[]{:S(2)}) collective-permute-start(bf16[2,2,160,768]{3,2,0,1:T(8,128)(2,1)} %copy.41), channel_id=1, source_target_pairs={{1,0},{2,1},{3,2},{5,4},{6,5},{7,6},{9,8},{10,9},{11,10},{13,12},{... | collective-permute-start | bytes 2949128 | tf_op jit(solution)/shard_map/ppermute | solution.py:206
  333.9 6.6 %copy-start = (bf16[2,640,768]{2,1,0:T(8,128)(2,1)S(1)}, bf16[2,640,768]{2,1,0:T(8,128)(2,1)}, u32[]{:S(2)}) copy-start(bf16[2,640,768]{2,1,0:T(8,128)(2,1)} %shard_map.85) | copy-start | bytes 5898244
  335.7 5.0 %copy-start.1 = (bf16[2,640,768]{2,1,0:T(8,128)(2,1)S(1)}, bf16[2,640,768]{2,1,0:T(8,128)(2,1)}, u32[]{:S(2)}) copy-start(bf16[2,640,768]{2,1,0:T(8,128)(2,1)} %shard_map.83) | copy-start | bytes 5898244
  335.8 26.7 %collective-permute-start.2 = (bf16[2,2,160,768]{3,2,0,1:T(8,128)(2,1)S(1)}, bf16[2,2,160,768]{3,2,0,1:T(8,128)(2,1)S(1)}, u32[]{:S(2)}, u32[]{:S(2)}) collective-permute-start(bf16[2,2,160,768]{3,2,0,1:T(8,128)(2,1)S(1)} %copy.36), channel_id=1, source_target_pairs={{0,1},{1,2},{2,3},{4,5},{5,6},{6,7},{8,9},{9,10},{10,11},{12,13},{... | collective-permute-start | bytes 2949128 | tf_op jit(solution)/shard_map/ppermute | solution.py:205
  341.9 25.7 %collective-permute-start.3 = (bf16[2,2,160,768]{3,2,0,1:T(8,128)(2,1)S(1)}, bf16[2,2,160,768]{3,2,0,1:T(8,128)(2,1)S(1)}, u32[]{:S(2)}, u32[]{:S(2)}) collective-permute-start(bf16[2,2,160,768]{3,2,0,1:T(8,128)(2,1)S(1)} %copy.37), channel_id=1, source_target_pairs={{1,0},{2,1},{3,2},{5,4},{6,5},{7,6},{9,8},{10,9},{11,10},{13,12},{... | collective-permute-start | bytes 2949128 | tf_op jit(solution)/shard_map/ppermute | solution.py:206
  346.8 5.1 %copy-start.2 = (bf16[2,2,160,768]{3,2,0,1:T(8,128)(2,1)}, bf16[2,2,160,768]{3,2,0,1:T(8,128)(2,1)S(1)}, u32[]{:S(2)}) copy-start(bf16[2,2,160,768]{3,2,0,1:T(8,128)(2,1)S(1)} %collective-permute-done.9) | copy-start | bytes 2949124
  348.3 46.6 %collective-permute-start.11 = (bf16[2,640,768]{2,1,0:T(8,128)(2,1)}, bf16[2,640,768]{2,1,0:T(8,128)(2,1)}, u32[]{:S(2)}, u32[]{:S(2)}) collective-permute-start(bf16[2,640,768]{2,1,0:T(8,128)(2,1)} %pad_maximum_fusion.3), channel_id=1, source_target_pairs={{4,0},{8,4},{12,8},{16,12},{20,16},{24,20},{28,24},{5,1},{9,5},{13... | collective-permute-start | bytes 5898248 | tf_op jit(solution)/shard_map/ppermute | solution.py:212
  362.5 6.7 %copy-start.4 = (bf16[2,2,160,768]{3,2,0,1:T(8,128)(2,1)}, bf16[2,2,160,768]{3,2,0,1:T(8,128)(2,1)S(1)}, u32[]{:S(2)}) copy-start(bf16[2,2,160,768]{3,2,0,1:T(8,128)(2,1)S(1)} %collective-permute-done.2) | copy-start | bytes 2949124
  362.5 48.3 %collective-permute-start.10 = (bf16[2,640,768]{2,1,0:T(8,128)(2,1)}, bf16[2,640,768]{2,1,0:T(8,128)(2,1)}, u32[]{:S(2)}, u32[]{:S(2)}) collective-permute-start(bf16[2,640,768]{2,1,0:T(8,128)(2,1)} %pad_maximum_fusion.2), channel_id=1, source_target_pairs={{0,4},{4,8},{8,12},{12,16},{16,20},{20,24},{24,28},{1,5},{5,9},{9,... | collective-permute-start | bytes 5898248 | tf_op jit(solution)/shard_map/ppermute | solution.py:211
  367.7 7.2 %copy-start.6 = (s32[16,16,80]{2,1,0:T(8,128)S(1)}, s32[16,16,80]{2,1,0:T(8,128)}, u32[]{:S(2)}) copy-start(s32[16,16,80]{2,1,0:T(8,128)} %param.15) | copy-start | bytes 245764
  367.7 7.3 %copy-start.9 = (s32[12,3]{0,1:T(4,128)S(1)}, s32[12,3]{0,1:T(4,128)}, u32[]{:S(2)}) copy-start(s32[12,3]{0,1:T(4,128)} %param.14) | copy-start | bytes 436
  369.2 57.3 %collective-permute-start.5 = (bf16[2,640,768]{2,1,0:T(8,128)(2,1)}, bf16[2,640,768]{2,1,0:T(8,128)(2,1)}, u32[]{:S(2)}, u32[]{:S(2)}) collective-permute-start(bf16[2,640,768]{2,1,0:T(8,128)(2,1)} %pad_maximum_fusion.1), channel_id=1, source_target_pairs={{4,0},{8,4},{12,8},{16,12},{20,16},{24,20},{28,24},{5,1},{9,5},{13... | collective-permute-start | bytes 5898248 | tf_op jit(solution)/shard_map/ppermute | solution.py:212
  372.5 65.3 %collective-permute-start.4 = (bf16[2,640,768]{2,1,0:T(8,128)(2,1)}, bf16[2,640,768]{2,1,0:T(8,128)(2,1)}, u32[]{:S(2)}, u32[]{:S(2)}) collective-permute-start(bf16[2,640,768]{2,1,0:T(8,128)(2,1)} %pad_maximum_fusion), channel_id=1, source_target_pairs={{0,4},{4,8},{8,12},{12,16},{16,20},{20,24},{24,28},{1,5},{5,9},{9,... | collective-permute-start | bytes 5898248 | tf_op jit(solution)/shard_map/ppermute | solution.py:211
  383.2 8.6 %copy-start.3 = (bf16[2,2,160,768]{3,2,0,1:T(8,128)(2,1)S(1)}, bf16[2,2,160,768]{3,2,0,1:T(8,128)(2,1)}, u32[]{:S(2)}) copy-start(bf16[2,2,160,768]{3,2,0,1:T(8,128)(2,1)} %copy-done.2) | copy-start | bytes 2949124
  390.9 2.0 copy-start.5
Sparse Core Ops, SparseCore 0:
  10.1 81.6 all-gather.10
  94.5 79.0 all-gather.6
  176.4 60.9 all-gather.8
  240.0 61.0 all-gather.4

commit v2 on v0

v2 whole, which is shorter than its diff:
```python
import functools

import jax
import jax.numpy as jnp
import numpy as np
from jax import lax
from jax.experimental import pallas as pl
from jax.experimental.pallas import tpu as pltpu
from jax.sharding import Mesh
from jax.sharding import PartitionSpec as P

HDIM = 128
HEADS = 12
TT = 1
TH = 2
TW = 8
CORES = 2
MATES = 4
OWN_HEADS = HEADS // MATES
SPAN = OWN_HEADS * HDIM
EPS = 1e-06
VMEM = 56 * 1024 * 1024
TEAM = ("pair", "core")


def swap(x, axis, flip):
    names = axis if isinstance(axis, tuple) else (axis,)
    count = int(np.prod([lax.axis_size(name) for name in names]))
    return lax.ppermute(x, axis, [(i, i ^ flip) for i in range(count)])


def swap_neighbours(x, axis, odd):
    count = lax.axis_size(axis)
    pairs = [(i, i + 1) for i in range(odd, count - 1, 2)]
    return lax.ppermute(x, axis, pairs + [(j, i) for i, j in pairs])


def modulate_body(tokens, scale, shift, out):
    values = tokens[...].astype(jnp.float32)
    centred = values - jnp.mean(values, axis=-1, keepdims=True)
    variance = jnp.mean(centred * centred, axis=-1, keepdims=True)
    normed = centred * lax.rsqrt(variance + EPS)
    out[...] = (normed * (1.0 + scale[...]) + shift[...]).astype(out.dtype)


def modulate(tokens, scale, shift):
    count, features = tokens.shape
    block = 128
    row = pl.BlockSpec((block, features), lambda i: (i, 0))
    whole = pl.BlockSpec((1, features), lambda i: (0, 0))
    return pl.pallas_call(
        modulate_body,
        grid=(count // block,),
        in_specs=[row, whole, whole],
        out_specs=row,
        out_shape=jax.ShapeDtypeStruct(tokens.shape, jnp.bfloat16),
        compiler_params=pltpu.CompilerParams(vmem_limit_bytes=VMEM),
        cost_estimate=pl.CostEstimate(
            flops=12 * count * features, bytes_accessed=4 * count * features, transcendentals=0
        ),
    )(tokens, scale.reshape(1, features), shift.reshape(1, features))


def project_body(places, order, *rest, arrays, steps, parts, normed):
    first, second = rest[:2]
    blocks = rest[2 : 2 + arrays]
    gain = rest[2 + arrays]
    out, weights, sems = rest[-3:]
    step = pl.program_id(0)
    pieces, depth, columns = blocks[0].shape

    @pl.when(step == 0)
    def _():
        copies = []
        for a in range(arrays):
            for p in range(pieces):
                row = pl.multiple_of(places[a * pieces + p] * depth, depth)
                copy = pltpu.make_async_copy(
                    blocks[a].at[p], weights.at[pl.ds(row, depth), :], sems.at[a * pieces + p]
                )
                copy.start()
                copies.append(copy)
        for copy in copies:
            copy.wait()

    def run(rows):
        wide = 2 * HDIM
        for start in range(0, columns, wide):
            stop = min(start + wide, columns)
            total = jnp.dot(rows[...], weights[:, start:stop], preferred_element_type=jnp.float32)
            for column in range(start, stop, HDIM):
                head = total[:, column - start : column - start + HDIM]
                part, offset = divmod(column, SPAN)
                if part < normed:
                    power = jnp.mean(head * head, axis=-1, keepdims=True)
                    head = head * lax.rsqrt(power + EPS) * gain[...]
                out[part, 0, :, offset : offset + HDIM] = head.astype(out.dtype)

    pl.when(step < steps)(lambda: run(first))
    pl.when(step >= steps)(lambda: run(second))


def project(first, second, order, blocks, places, gain, parts, normed, members, onto=None):
    rows, depth = first.shape
    pieces, shard, columns = blocks[0].shape
    arrays = len(blocks)
    block = rows // 2
    steps = rows // block
    specs = [
        pl.BlockSpec((block, depth), lambda i, p, o: (jnp.minimum(i, steps - 1), 0)),
        pl.BlockSpec((block, depth), lambda i, p, o: (jnp.maximum(i - steps, 0), 0)),
    ]
    specs += [pl.BlockSpec(memory_space=pl.ANY)] * arrays
    specs += [pl.BlockSpec((1, HDIM), lambda i, p, o: (0, 0))]
    operands = [places, order, first, second, *blocks, gain.reshape(1, HDIM)]
    aliases = {}
    if onto is not None:
        specs.append(pl.BlockSpec(memory_space=pl.ANY))
        operands.append(onto)
        aliases = {len(operands) - 1: 0}
    return pl.pallas_call(
        functools.partial(project_body, arrays=arrays, steps=steps, parts=parts, normed=normed),
        grid_spec=pltpu.PrefetchScalarGridSpec(
            num_scalar_prefetch=2,
            grid=(2 * steps,),
            in_specs=specs,
            out_specs=pl.BlockSpec(
                (parts, 1, block, SPAN), lambda i, p, o: (0, o[i // steps], i % steps, 0)
            ),
            scratch_shapes=[
                pltpu.VMEM((depth, columns), jnp.bfloat16),
                pltpu.SemaphoreType.DMA((arrays * pieces,)),
            ],
        ),
        out_shape=jax.ShapeDtypeStruct((parts, members, rows, SPAN), jnp.bfloat16),
        input_output_aliases=aliases,
        compiler_params=pltpu.CompilerParams(vmem_limit_bytes=VMEM),
        cost_estimate=pl.CostEstimate(
            flops=4 * rows * depth * columns,
            bytes_accessed=2 * depth * columns + 4 * rows * depth + 4 * rows * columns,
            transcendentals=0,
        ),
    )(*operands)


def attend_body(meta, *rest, near, chip_frames, frames, cell, inner, sides):
    query = rest[0]
    chips = (rest[1:4], rest[4:7])
    borders = [rest[7 + 2 * s : 9 + 2 * s] for s in range(sides)]
    valid = rest[7 + 2 * sides]
    out, keys, values, band = rest[-4:]
    head_step, frame = pl.program_id(0), pl.program_id(1)
    member, pair, z_odd, r_odd = (meta[3 * HEADS + i] for i in range(4))
    head = member * OWN_HEADS + head_step
    width = cell // TH

    @pl.when((head_step == 0) & (frame == 0))
    def _():
        values[:, :, HDIM:] = valid[...]
        q_tile = lax.broadcasted_iota(jnp.int32, (cell, 3 * cell), 0)
        k_tile = lax.broadcasted_iota(jnp.int32, (cell, 3 * cell), 1)
        apart = jnp.abs(lax.rem(q_tile, width) // TW - lax.rem(k_tile, width) // TW)
        for reach in range(3):
            band[reach] = jnp.where(apart <= reach, 1.0, 0.0).astype(band.dtype)
        if sides < 2:
            empty = jnp.where(r_odd == 1, frames + 1, 0)
            keys[empty] = jnp.zeros(keys.shape[1:], keys.dtype)
            values[empty, :, :HDIM] = jnp.zeros((keys.shape[1], HDIM), values.dtype)

    @pl.when(frame == 0)
    def _():
        even_rows = pl.multiple_of(jnp.where(z_odd == 1, 0, cell + inner), cell)
        odd_rows = pl.multiple_of(jnp.where(z_odd == 1, cell + inner, 0), cell)

        def put(place, start, length, key, value):
            rows = pl.ds(start, length)
            keys[place, rows, :] = key
            values[place, rows, :HDIM] = value * valid[place, rows, :]

        for which, (own, even, odd) in enumerate(chips):
            base = 1 + chip_frames * (pair if which == 0 else 1 - pair)
            for index in range(chip_frames):
                put(base + index, cell, inner, own[0, index], own[1, index])
                put(base + index, even_rows, cell, even[0, index], even[1, index])
                put(base + index, odd_rows, cell, odd[0, index], odd[1, index])
        for side, (own, ends) in enumerate(borders):
            place = jnp.where(r_odd == 1 - side, 0, frames + 1) if side == 0 else jnp.where(r_odd == 1, frames + 1, 0)
            put(place, cell, inner, own[0], own[1])
            put(place, even_rows, cell, ends[0, 0], ends[0, 1])
            put(place, odd_rows, cell, ends[1, 0], ends[1, 1])

    scale = np.float32(np.log2(np.e) / np.sqrt(HDIM))
    reach_t, reach_h, reach_w = (meta[3 * head + i] for i in range(3))

    def attend(over_t, over_h):
        seen = (3 if over_h else 1) * cell
        mask = band[reach_w, :, :seen]
        for tile in range(inner // cell):
            rows = pl.ds((tile + (0 if over_h else 1)) * cell, seen)
            mine = query[0, 0, 0, pl.ds(tile * cell, cell), :]
            total = None
            for step in (0, 1, 2) if over_t else (1,):
                scores = lax.dot_general(
                    mine,
                    keys[frame + step, rows, :],
                    (((1,), (1,)), ((), ())),
                    preferred_element_type=jnp.float32,
                )
                terms = jnp.exp2(scores * scale).astype(jnp.bfloat16) * mask
                part = jnp.dot(terms, values[frame + step, rows, :], preferred_element_type=jnp.float32)
                total = part if total is None else total + part
            here = valid[frame + 1, pl.ds((tile + 1) * cell, cell), :] > 0
            weight = jnp.where(here, total[:, HDIM:], 1.0)
            result = jnp.where(here, total[:, :HDIM] / weight, 0.0)
            out[0, 0, pl.ds(tile * cell, cell), :] = result.astype(out.dtype)

    for over_t in (False, True):
        for over_h in (False, True):
            pl.when(((reach_t > 0) == over_t) & ((reach_h > 0) == over_h))(
                functools.partial(attend, over_t, over_h)
            )


def attend(meta, query, chips, borders, valid, near):
    _, chip_frames, inner, _ = chips[0][0].shape
    frames = 2 * chip_frames
    cell = chips[0][1].shape[2]
    span = inner + 2 * cell
    head = lambda h, f, m: (0, 0, 0, h)
    specs = [
        pl.BlockSpec((1, 1, 1, inner, HDIM), lambda h, f, m: (0, f // near, f % near, 0, h)),
    ]
    operands = [query]
    for own, even, odd in chips:
        for part in (own, even, odd):
            specs.append(pl.BlockSpec((*part.shape[:-1], HDIM), head))
            operands.append(part)
    for own, ends in borders:
        specs.append(pl.BlockSpec((*own.shape[:-1], HDIM), lambda h, f, m: (0, 0, h)))
        specs.append(pl.BlockSpec((*ends.shape[:-1], HDIM), head))
        operands += [own, ends]
    specs.append(pl.BlockSpec(valid.shape, lambda h, f, m: (0, 0, 0)))
    operands.append(valid)
    flips = lambda f, m: (f // near) ^ m[3 * HEADS]
    return pl.pallas_call(
        functools.partial(
            attend_body,
            near=near,
            chip_frames=chip_frames,
            frames=frames,
            cell=cell,
            inner=inner,
            sides=len(borders),
        ),
        grid_spec=pltpu.PrefetchScalarGridSpec(
            num_scalar_prefetch=1,
            grid=(OWN_HEADS, frames),
            in_specs=specs,
            out_specs=pl.BlockSpec((1, 1, inner, HDIM), lambda h, f, m: (flips(f, m), f % near, 0, h)),
            scratch_shapes=[
                pltpu.VMEM((frames + 2, span, HDIM), jnp.bfloat16),
                pltpu.VMEM((frames + 2, span, 2 * HDIM), jnp.bfloat16),
                pltpu.VMEM((3, cell, 3 * cell), jnp.bfloat16),
            ],
        ),
        out_shape=jax.ShapeDtypeStruct((MATES, near, inner, SPAN), jnp.bfloat16),
        compiler_params=pltpu.CompilerParams(vmem_limit_bytes=VMEM),
        cost_estimate=pl.CostEstimate(
            flops=OWN_HEADS * frames * inner * 9 * cell * HDIM * 6,
            bytes_accessed=2 * OWN_HEADS * HDIM * frames * (2 * inner + 2 * span),
            transcendentals=OWN_HEADS * frames * inner * 9 * cell,
        ),
    )(meta, *operands)


def collect_body(member, *rest):
    out = rest[-1]
    for flip, piece in enumerate(rest[:-1]):
        column = pl.multiple_of((member[0] ^ flip) * SPAN, SPAN)
        out[:, pl.ds(column, SPAN)] = piece[...]


def collect(member, pieces):
    rows = pieces[0].shape[0]
    whole = pl.BlockSpec((rows, SPAN), lambda i, m: (0, 0))
    return pl.pallas_call(
        collect_body,
        grid_spec=pltpu.PrefetchScalarGridSpec(
            num_scalar_prefetch=1,
            grid=(1,),
            in_specs=[whole] * MATES,
            out_specs=pl.BlockSpec((rows, HEADS * HDIM), lambda i, m: (0, 0)),
        ),
        out_shape=jax.ShapeDtypeStruct((rows, HEADS * HDIM), jnp.bfloat16),
        compiler_params=pltpu.CompilerParams(vmem_limit_bytes=VMEM),
    )(member.reshape(1), *pieces)


def gather_blocks(pieces):
    lines = [pieces] + [swap(pieces, "height", d) for d in range(1, lax.axis_size("height"))]
    found = list(lines)
    for e in range(1, lax.axis_size("rest")):
        found += [swap(line, "rest", e) for line in lines]
    return found


def aligned(blocks, places):
    shard = blocks[0].shape[1]
    if shard % 16 == 0:
        return blocks, places
    rows = jnp.concatenate(blocks, axis=0)
    ordered = jnp.zeros_like(rows).at[places].set(rows)
    return [ordered.reshape(1, -1, rows.shape[-1])], jnp.zeros((1,), jnp.int32)


def per_device(tokens, mod_scale, mod_shift, w_qkv, q_gain, k_gain, window, valid):
    frames, rows, width, features = tokens.shape
    count = frames * rows * width
    inner = rows * width
    cell = TH * width
    model = w_qkv.shape[1] // 3
    rest, pair, core, height = (lax.axis_index(a) for a in ("rest", "pair", "core", "height"))
    member = pair * CORES + core
    high = lax.axis_size("height")
    many = lax.axis_size("rest")

    def columns_of(mate):
        return jnp.concatenate(
            [lax.dynamic_slice_in_dim(w_qkv, s * model + mate * SPAN, SPAN, axis=1) for s in range(3)], axis=1
        )

    shares = [columns_of(member)] + [swap(columns_of(member ^ flip), TEAM, flip) for flip in range(1, MATES)]
    stacked = jnp.stack(shares)
    kv_blocks = gather_blocks(stacked[:, :, SPAN:])
    q_blocks = gather_blocks(stacked[:, :, :SPAN])
    places = jnp.stack(
        [
            ((rest ^ e) * MATES + (member ^ j)) * high + (height ^ d)
            for e in range(many)
            for d in range(high)
            for j in range(MATES)
        ]
    ).astype(jnp.int32)
    kv_blocks, kv_places = aligned(kv_blocks, places)
    q_blocks, q_places = aligned(q_blocks, places)

    mine = modulate(tokens.reshape(count, features), mod_scale, mod_shift)
    across = swap(mine, "pair", 1)
    beside = swap(mine, "core", 1)
    beyond = swap(across, "core", 1)

    z_odd = height % 2
    r_odd = rest % 2
    orders = jnp.stack([core, 1 - core]).astype(jnp.int32)

    def chip_cells(first, second):
        kv = project(first, second, orders, kv_blocks, kv_places, k_gain, 2, 1, CORES)
        grid = kv.reshape(2, CORES * frames, inner, SPAN)
        low, top = jnp.int32(0), jnp.int32(inner - cell)
        even = swap_neighbours(
            lax.dynamic_slice_in_dim(grid, jnp.where(z_odd == 1, low, top), cell, axis=2), "height", 0
        )
        odd = swap_neighbours(
            lax.dynamic_slice_in_dim(grid, jnp.where(z_odd == 1, top, low), cell, axis=2), "height", 1
        )
        return grid, even, odd

    near_chip = chip_cells(mine, beside)
    far_chip = chip_cells(across, beyond)
    mates = jnp.stack([member ^ j for j in range(MATES)]).astype(jnp.int32)
    query = project(mine, beside, mates[:2], q_blocks, q_places, q_gain, 1, 1, MATES)
    query = project(across, beyond, mates[2:], q_blocks, q_places, q_gain, 1, 1, MATES, query)

    def border(odd):
        last = r_odd == odd
        chosen = jnp.where(last, 1, 0) == pair
        frame = jnp.where(last, CORES * frames - 1, 0)
        own, even, other = (
            jnp.where(
                chosen,
                lax.dynamic_index_in_dim(a, frame, 1, False),
                lax.dynamic_index_in_dim(b, frame, 1, False),
            )
            for a, b in zip(near_chip, far_chip)
        )
        return (
            swap_neighbours(own, "rest", odd),
            swap_neighbours(jnp.stack([even, other]), "rest", odd),
        )

    borders = [border(odd) for odd in range(min(2, many - 1))]

    total_frames = MATES * frames
    valid_pad = jnp.pad(valid, ((TT, TT), (TH, TH), (0, 0)))
    around = lax.dynamic_slice(
        valid_pad,
        (rest * total_frames, height * rows, jnp.int32(0)),
        (total_frames + 2 * TT, rows + 2 * TH, width),
    )
    seen = jnp.broadcast_to(
        (around > 0).astype(jnp.bfloat16).reshape(total_frames + 2 * TT, -1, 1),
        (total_frames + 2 * TT, (rows + 2 * TH) * width, HDIM),
    )
    meta = jnp.concatenate(
        [window.reshape(-1), jnp.stack([member, pair, z_odd, r_odd]).astype(jnp.int32)]
    )
    queries = query.reshape(1, MATES, frames, inner, SPAN)
    attended = attend(meta, queries, (near_chip, far_chip), borders, seen, frames)
    attended = attended.reshape(MATES, count, SPAN)
    pieces = [attended[0]] + [swap(attended[flip], TEAM, flip) for flip in range(1, MATES)]
    return collect(member.astype(jnp.int32), pieces).reshape(frames, rows, width, model)


def solution(mesh):
    split = Mesh(
        mesh.devices.reshape(mesh.shape["tm"] // MATES, MATES // CORES, CORES, mesh.shape["height"]),
        ("rest", "pair", "core", "height"),
    )
    along = ("rest", "pair", "core")
    in_specs = (
        P(along, "height", None, None),
        P(),
        P(),
        P((*along, "height"), None),
        P(),
        P(),
        P(),
        P(),
    )
    out_specs = P(along, "height", None, None)
    return jax.shard_map(
        per_device, mesh=split, in_specs=in_specs, out_specs=out_specs, check_vma=False
    )
```

time: 597 us -> 423 us (0.71)
  matrix products: 157 us -> 0 us
  Pallas kernels: 0 us -> 91.3 us
  local copies, waits for them, and re-layouts: 97.9 us -> 22.9 us
  other arithmetic: 35.9 us -> 5.55 us
  starting transfers between devices: 11.3 us -> 28.4 us
  between operations: 13.7 us -> 0.28 us
    all_gather x1 -> x0, waiting for transfers between devices: 163 us -> none  [per_device(): full_weight = lax.all_gather(w_qkv, ('tm', 'height'), axis=0, tiled=True)]
    ppermute x4 -> x29, waiting for transfers between devices: 110 us -> 270 us  [the longest x23 270 us: swap(): return lax.ppermute(x, axis, [(i, i ^ flip) for i in range(count)])]
    dot_general x25 -> x0, matrix products: 157 us -> none  [the longest x12 107 us: per_head(): jnp.einsum('qd,kd->qk', query_one, key_one, preferred_element_type=jnp.fl...]
    pallas_call x0 -> x7, Pallas kernels: none -> 91.3 us  [the longest x4 49.9 us: project(): pl.pallas_call(functools.partial(project_body, arrays=arrays, steps=steps...]
    squeeze x2 -> x0, local copies, waits for them, and re-layouts: 30.2 us -> none  [the longest x1 15.1 us: per_device(): key_heads = jnp.transpose(extended[0], (1, 0, 2))]
    slice x16 -> x1, local copies, waits for them, and re-layouts: 21.9 us -> 2.49 us  [per_device(): attended[flip]]
    ppermute x4 -> x29, starting transfers between devices: 11.3 us -> 28.4 us  [the longest x23 20.5 us: swap(): return lax.ppermute(x, axis, [(i, i ^ flip) for i in range(count)])]
    unnamed x34 -> x55, local copies, waits for them, and re-layouts: 23.1 us -> 7.02 us
  transfers between devices with their start and end apart: 5 -> 29, of which waited for: 4 -> 18; matrix products, arithmetic and copies ran while one was open for 4% -> 4% of each run, Pallas kernels for 0% -> 9%
where the time goes in v2:
time: 423 us; the launch traced here: 418 us
  waiting for transfers between devices  270 us (64%)
  Pallas kernels  91.3 us (22%)
  starting transfers between devices  28.4 us (7%)
  local copies, waits for them, and re-layouts  22.9 us (5%)
  other arithmetic  5.55 us (1%)
    ppermute x23, waiting for transfers between devices, swap(): return lax.ppermute(x, axis, [(i, i ^ flip) for i in range(count)])  270 us
    pallas_call x4, Pallas kernels, project(): pl.pallas_call(functools.partial(project_body, arrays=arrays, steps=steps...  49.9 us
    pallas_call x1, Pallas kernels, attend(): pl.pallas_call(functools.partial(attend_body, near=near, chip_frames=chip...  31.6 us
    ppermute x23, starting transfers between devices, swap(): return lax.ppermute(x, axis, [(i, i ^ flip) for i in range(count)])  20.5 us
  transfers between devices with their start and end apart: 29, of which 18 were waited for; matrix products, arithmetic and copies ran while one was open for 4% of the time, Pallas kernels for 9%

profile of v2, /device:TPU:4, one launch (start us, length us, event | category | flops | bytes accessed | tf_op | source)
XLA Modules:
  0.0 418.0 jit_solution(18172807111211654881)
XLA Ops:
  0.0 6.8 %shard_map.82.rest_0_ = bf16[640,3072]{1,0:T(8,128)(2,1)} custom-call(bf16[640,3072]{1,0:T(8,128)(2,1)} %bitcast.72, f32[1,3072]{1,0:T(1,128)} %bitcast.89, f32[1,3072]{1,0:T(1,128)} %bitcast.90), custom_call_target="tpu_custom_call" | custom-call | flops 23592960 | bytes 7864320 | tf_op jit(solution)/shard_map/pallas_call | solution.py:51
  6.8 1.5 collective-permute-start
  8.3 85.5 %collective-permute-done.rest_0_ = bf16[640,3072]{1,0:T(8,128)(2,1)} collective-permute-done((bf16[640,3072]{1,0:T(8,128)(2,1)}, bf16[640,3072]{1,0:T(8,128)(2,1)}, u32[]{:S(2)}, u32[]{:S(2)}) %collective-permute-start) | collective-permute-done | bytes 3932192 | tf_op jit(solution)/shard_map/ppermute | solution.py:29
  94.5 1.6 collective-permute-start.3
  96.2 4.3 %collective-permute-done.2 = bf16[96,1152]{1,0:T(8,128)(2,1)S(1)} collective-permute-done((bf16[96,1152]{1,0:T(8,128)(2,1)S(1)}, bf16[96,1152]{1,0:T(8,128)(2,1)S(1)}, u32[]{:S(2)}, u32[]{:S(2)}) %collective-permute-start.2) | collective-permute-done | bytes 221216 | tf_op jit(solution)/shard_map/ppermute | solution.py:29
  100.5 2.3 collective-permute-done.3
  102.9 2.9 collective-permute-done.4
  106.4 3.6 collective-permute-start.15
  110.0 11.8 %collective-permute-done.16.rest_6_ = bf16[4,96,768]{2,1,0:T(8,128)(2,1)S(1)} collective-permute-done((bf16[4,96,768]{2,1,0:T(8,128)(2,1)S(1)}, bf16[4,96,768]{2,1,0:T(8,128)(2,1)S(1)}, u32[]{:S(2)}, u32[]{:S(2)}) %collective-permute-start.16) | collective-permute-done | bytes 589856 | tf_op jit(solution)/shard_map/ppermute | solution.py:29
  121.9 1.6 collective-permute-start.13
  123.4 1.1 collective-permute-done.15.rest_5_
  124.5 1.4 collective-permute-start.19
  125.9 35.4 %collective-permute-done.14.rest_4_ = bf16[4,96,768]{2,1,0:T(8,128)(2,1)S(1)} collective-permute-done((bf16[4,96,768]{2,1,0:T(8,128)(2,1)S(1)}, bf16[4,96,768]{2,1,0:T(8,128)(2,1)S(1)}, u32[]{:S(2)}, u32[]{:S(2)}) %collective-permute-start.14) | collective-permute-done | bytes 589856 | tf_op jit(solution)/shard_map/ppermute | solution.py:29
  161.4 1.2 collective-permute-start.18
  164.7 13.0 %collective-permute-done.18.rest_8_ = bf16[4,96,768]{2,1,0:T(8,128)(2,1)} collective-permute-done((bf16[4,96,768]{2,1,0:T(8,128)(2,1)S(1)}, bf16[4,96,768]{2,1,0:T(8,128)(2,1)}, u32[]{:S(2)}, u32[]{:S(2)}) %collective-permute-start.18) | collective-permute-done | bytes 589856 | tf_op jit(solution)/shard_map/ppermute | solution.py:29
  177.7 11.6 %collective-permute-done.17.rest_7_ = bf16[4,96,768]{2,1,0:T(8,128)(2,1)} collective-permute-done((bf16[4,96,768]{2,1,0:T(8,128)(2,1)S(1)}, bf16[4,96,768]{2,1,0:T(8,128)(2,1)}, u32[]{:S(2)}, u32[]{:S(2)}) %collective-permute-start.17) | collective-permute-done | bytes 589856 | tf_op jit(solution)/shard_map/ppermute | solution.py:29
  189.3 13.7 %shard_map.85 = bf16[2,2,640,384]{3,2,1,0:T(8,128)(2,1)} custom-call(s32[32]{0:T(128)} %stack.188.places, s32[2]{0:T(128)} %pad_add_fusion.2.order, bf16[640,3072]{1,0:T(8,128)(2,1)} %shard_map.82.rest_0_, bf16[640,3072]{1,0:T(8,128)(2,1)} %collective-permute-done.12.rest_1_, bf16[4,96,768]{2,1,0:T(8,128)(2,1)} %copy-done.14, ...), custom_call_target="tpu_custom_call" | custom-call | flops 6039797760 | bytes 14548992 | tf_op jit(solution)/shard_map/pallas_call | solution.py:121
  203.0 13.8 %shard_map.86 = bf16[2,2,640,384]{3,2,1,0:T(8,128)(2,1)} custom-call(s32[32]{0:T(128)} %stack.188.places, s32[2]{0:T(128)} %pad_add_fusion.2.order, bf16[640,3072]{1,0:T(8,128)(2,1)} %collective-permute-done.rest_0_, bf16[640,3072]{1,0:T(8,128)(2,1)} %collective-permute-done.1.rest_1_, bf16[4,96,768]{2,1,0:T(8,128)(2,1)} %copy-done.14, ...), custom_call_target="tpu_custom_call" | custom-call | flops 6039797760 | bytes 14548992 | tf_op jit(solution)/shard_map/pallas_call | solution.py:121
  216.8 2.0 constant_dynamic-slice_fusion
  221.0 1.1 copy.29
  222.9 3.4 collective-permute-start.20
  226.5 1.4 collective-permute-start.7
  227.9 1.1 copy.31
  229.0 1.6 collective-permute-start.23
  230.6 45.4 %collective-permute-done.7.rest_5_ = bf16[4,96,384]{2,1,0:T(8,128)(2,1)S(1)} collective-permute-done((bf16[4,96,384]{2,1,0:T(8,128)(2,1)S(1)}, bf16[4,96,384]{2,1,0:T(8,128)(2,1)S(1)}, u32[]{:S(2)}, u32[]{:S(2)}) %collective-permute-start.7) | collective-permute-done | bytes 294944 | tf_op jit(solution)/shard_map/ppermute | solution.py:29
  276.9 16.8 %collective-permute-done.6.rest_4_ = bf16[4,96,384]{2,1,0:T(8,128)(2,1)} collective-permute-done((bf16[4,96,384]{2,1,0:T(8,128)(2,1)S(1)}, bf16[4,96,384]{2,1,0:T(8,128)(2,1)}, u32[]{:S(2)}, u32[]{:S(2)}) %collective-permute-start.6) | collective-permute-done | bytes 294944 | tf_op jit(solution)/shard_map/ppermute | solution.py:29
  295.9 1.1 fusion
  297.0 4.1 collective-permute-done.5.rest_3_
  304.1 1.1 collective-permute-start.9
  305.2 1.1 select_bitcast_fusion.1
  306.3 1.1 collective-permute-start.24
  308.4 2.6 collective-permute-done.8.rest_6_
  312.0 5.3 %collective-permute-done.11.rest_9_ = bf16[4,96,384]{2,1,0:T(8,128)(2,1)S(1)} collective-permute-done((bf16[4,96,384]{2,1,0:T(8,128)(2,1)}, bf16[4,96,384]{2,1,0:T(8,128)(2,1)S(1)}, u32[]{:S(2)}, u32[]{:S(2)}) %collective-permute-start.11) | collective-permute-done | bytes 294944 | tf_op jit(solution)/shard_map/ppermute | solution.py:29
  317.4 6.3 %collective-permute-done.10.rest_8_ = bf16[4,96,384]{2,1,0:T(8,128)(2,1)S(1)} collective-permute-done((bf16[4,96,384]{2,1,0:T(8,128)(2,1)}, bf16[4,96,384]{2,1,0:T(8,128)(2,1)S(1)}, u32[]{:S(2)}, u32[]{:S(2)}) %collective-permute-start.10) | collective-permute-done | bytes 294944 | tf_op jit(solution)/shard_map/ppermute | solution.py:29
  323.7 6.3 %collective-permute-done.9.rest_7_ = bf16[4,96,384]{2,1,0:T(8,128)(2,1)S(1)} collective-permute-done((bf16[4,96,384]{2,1,0:T(8,128)(2,1)}, bf16[4,96,384]{2,1,0:T(8,128)(2,1)S(1)}, u32[]{:S(2)}, u32[]{:S(2)}) %collective-permute-start.9) | collective-permute-done | bytes 294944 | tf_op jit(solution)/shard_map/ppermute | solution.py:29
  330.7 11.2 %shard_map.83.rest_11_ = bf16[1,4,640,384]{3,2,1,0:T(8,128)(2,1)} custom-call(s32[32]{0:T(128)} %stack.188.places, s32[2]{0:T(128)} %get-tuple-element.26.order, bf16[640,3072]{1,0:T(8,128)(2,1)} %shard_map.82.rest_0_, bf16[640,3072]{1,0:T(8,128)(2,1)} %collective-permute-done.12.rest_1_, bf16[4,96,384]{2,1,0:T(8,128)(2,1)} %copy-done.1, ...), custom_call_target="tpu_custom_call" | custom-call | flops 3019898880 | bytes 11206656 | tf_op jit(solution)/shard_map/pallas_call | solution.py:121
  342.0 11.2 %shard_map.84 = bf16[1,4,640,384]{3,2,1,0:T(8,128)(2,1)} custom-call(s32[32]{0:T(128)} %stack.188.places, s32[2]{0:T(128)} %get-tuple-element.25.order, bf16[640,3072]{1,0:T(8,128)(2,1)} %collective-permute-done.rest_0_, bf16[640,3072]{1,0:T(8,128)(2,1)} %collective-permute-done.1.rest_1_, ...), custom_call_target="tpu_custom_call", output_to_operand_aliasing={{}: (13, {})} | custom-call | flops 3019898880 | bytes 11206656 | tf_op jit(solution)/shard_map/pallas_call | solution.py:121
  353.2 1.1 copy.25.rest_3_
  354.3 2.3 copy.24.rest_2_
  356.5 2.3 copy.26.rest_5_
  358.8 2.3 copy.27.rest_6_
  361.1 1.9 broadcast_in_dim.12.rest_9_
  363.1 31.6 %shard_map.87 = bf16[4,2,320,384]{3,2,1,0:T(8,128)(2,1)} custom-call(s32[40]{0:T(128)} %concatenate.17.meta, bf16[1,4,2,320,384]{4,3,2,1,0:T(8,128)(2,1)} %bitcast.71, bf16[2,4,320,384]{3,2,1,0:T(8,128)(2,1)} %bitcast.73, bf16[2,4,160,384]{3,2,1,0:T(8,128)(2,1)} %copy.24.rest_2_, bf16[2,4,160,384]{3,2,1,0:T(8,128)(2,1)} %copy.25.rest_3_, ...), custom_call_target="tpu_custom_call" | custom-call | flops 8493465600 | bytes 11796480 | tf_op jit(solution)/shard_map/pallas_call | solution.py:245
  394.7 2.5 fusion.3
  397.2 2.1 collective-permute-start.26
  399.3 11.4 %collective-permute-done.27.rest_2_ = bf16[640,384]{1,0:T(8,128)(2,1)S(1)} collective-permute-done((bf16[640,384]{1,0:T(8,128)(2,1)S(1)}, bf16[640,384]{1,0:T(8,128)(2,1)S(1)}, u32[]{:S(2)}, u32[]{:S(2)}) %collective-permute-start.27) | collective-permute-done | bytes 491552 | tf_op jit(solution)/shard_map/ppermute | solution.py:29
  410.8 3.3 collective-permute-done.28.rest_3_
  415.1 2.9 shard_map.88
  (97 shorter events, 16.6 us)
Async XLA Ops:
  0.0 93.8 %copy-start.7 = (bf16[96,4608]{1,0:T(8,128)(2,1)S(1)}, bf16[96,4608]{1,0:T(8,128)(2,1)}, u32[]{:S(2)}) copy-start(bf16[96,4608]{1,0:T(8,128)(2,1)} %param.11) | copy-start | bytes 2654212
  6.8 87.0 %collective-permute-start = (bf16[640,3072]{1,0:T(8,128)(2,1)}, bf16[640,3072]{1,0:T(8,128)(2,1)}, u32[]{:S(2)}, u32[]{:S(2)}) collective-permute-start(bf16[640,3072]{1,0:T(8,128)(2,1)} %shard_map.82.rest_0_), channel_id=1, source_target_pairs={{0,8},{8,0},{1,9},{9,1},{2,10},{10,2},{3,11},{11,3},{4,12},{12,4},... | collective-permute-start | bytes 11796488 | tf_op jit(solution)/shard_map/ppermute | solution.py:29
  8.3 181.0 %collective-permute-start.12 = (bf16[640,3072]{1,0:T(8,128)(2,1)}, bf16[640,3072]{1,0:T(8,128)(2,1)}, u32[]{:S(2)}, u32[]{:S(2)}) collective-permute-start(bf16[640,3072]{1,0:T(8,128)(2,1)} %shard_map.82.rest_0_), channel_id=1, source_target_pairs={{0,4},{4,0},{1,5},{5,1},{2,6},{6,2},{3,7},{7,3},{8,12},{12,8},{9,1... | collective-permute-start | bytes 11796488 | tf_op jit(solution)/shard_map/ppermute | solution.py:29
  93.8 109.2 %collective-permute-start.1 = (bf16[640,3072]{1,0:T(8,128)(2,1)}, bf16[640,3072]{1,0:T(8,128)(2,1)}, u32[]{:S(2)}, u32[]{:S(2)}) collective-permute-start(bf16[640,3072]{1,0:T(8,128)(2,1)} %collective-permute-done.rest_0_), channel_id=1, source_target_pairs={{0,4},{4,0},{1,5},{5,1},{2,6},{6,2},{3,7},{7,3},{8,12},{12,8},{9,1... | collective-permute-start | bytes 11796488 | tf_op jit(solution)/shard_map/ppermute | solution.py:29
  93.9 6.6 %collective-permute-start.2 = (bf16[96,1152]{1,0:T(8,128)(2,1)S(1)}, bf16[96,1152]{1,0:T(8,128)(2,1)S(1)}, u32[]{:S(2)}, u32[]{:S(2)}) collective-permute-start(bf16[96,1152]{1,0:T(8,128)(2,1)S(1)} %pad_maximum_fusion.5), channel_id=1, source_target_pairs={{0,4},{4,0},{8,12},{12,8},{1,5},{5,1},{9,13},{13,9},{2,6},{6,2},{1... | collective-permute-start | bytes 663560 | tf_op jit(solution)/shard_map/ppermute | solution.py:29
  94.5 8.4 %collective-permute-start.3 = (bf16[96,1152]{1,0:T(8,128)(2,1)S(1)}, bf16[96,1152]{1,0:T(8,128)(2,1)S(1)}, u32[]{:S(2)}, u32[]{:S(2)}) collective-permute-start(bf16[96,1152]{1,0:T(8,128)(2,1)S(1)} %pad_maximum_fusion.6), channel_id=1, source_target_pairs={{0,8},{4,12},{8,0},{12,4},{1,9},{5,13},{9,1},{13,5},{2,10},{6,14},... | collective-permute-start | bytes 663560 | tf_op jit(solution)/shard_map/ppermute | solution.py:29
  96.1 9.6 %collective-permute-start.4 = (bf16[96,1152]{1,0:T(8,128)(2,1)S(1)}, bf16[96,1152]{1,0:T(8,128)(2,1)S(1)}, u32[]{:S(2)}, u32[]{:S(2)}) collective-permute-start(bf16[96,1152]{1,0:T(8,128)(2,1)S(1)} %pad_maximum_fusion.7), channel_id=1, source_target_pairs={{0,12},{4,8},{8,4},{12,0},{1,13},{5,9},{9,5},{13,1},{2,14},{6,10},... | collective-permute-start | bytes 663560 | tf_op jit(solution)/shard_map/ppermute | solution.py:29
  100.5 5.2 %copy-start.8 = (bf16[96,1152]{1,0:T(8,128)(2,1)}, bf16[96,1152]{1,0:T(8,128)(2,1)S(1)}, u32[]{:S(2)}) copy-start(bf16[96,1152]{1,0:T(8,128)(2,1)S(1)} %collective-permute-done.2) | copy-start | bytes 663556
  102.9 2.9 copy-start.10
  105.8 83.5 %copy-start.14 = (bf16[4,96,768]{2,1,0:T(8,128)(2,1)}, bf16[4,96,768]{2,1,0:T(8,128)(2,1)S(1)}, u32[]{:S(2)}) copy-start(bf16[4,96,768]{2,1,0:T(8,128)(2,1)S(1)} %pad_maximum_fusion.rest_2_) | copy-start | bytes 1769476
  105.8 16.1 %collective-permute-start.16 = (bf16[4,96,768]{2,1,0:T(8,128)(2,1)S(1)}, bf16[4,96,768]{2,1,0:T(8,128)(2,1)S(1)}, u32[]{:S(2)}, u32[]{:S(2)}) collective-permute-start(bf16[4,96,768]{2,1,0:T(8,128)(2,1)S(1)} %pad_maximum_fusion.rest_2_), channel_id=1, source_target_pairs={{0,16},{16,0},{1,17},{17,1},{2,18},{18,2},{3,19},{19,3},{4,20},{20... | collective-permute-start | bytes 1769480 | tf_op jit(solution)/shard_map/ppermute | solution.py:29
  106.4 18.1 %collective-permute-start.15 = (bf16[4,96,768]{2,1,0:T(8,128)(2,1)S(1)}, bf16[4,96,768]{2,1,0:T(8,128)(2,1)S(1)}, u32[]{:S(2)}, u32[]{:S(2)}) collective-permute-start(bf16[4,96,768]{2,1,0:T(8,128)(2,1)S(1)} %pad_maximum_fusion.rest_2_), channel_id=1, source_target_pairs={{0,3},{1,2},{2,1},{3,0},{4,7},{5,6},{6,5},{7,4},{8,11},{9,10},{10,... | collective-permute-start | bytes 1769480 | tf_op jit(solution)/shard_map/ppermute | solution.py:29
  110.0 51.3 %collective-permute-start.14 = (bf16[4,96,768]{2,1,0:T(8,128)(2,1)S(1)}, bf16[4,96,768]{2,1,0:T(8,128)(2,1)S(1)}, u32[]{:S(2)}, u32[]{:S(2)}) collective-permute-start(bf16[4,96,768]{2,1,0:T(8,128)(2,1)S(1)} %pad_maximum_fusion.rest_2_), channel_id=1, source_target_pairs={{0,2},{1,3},{2,0},{3,1},{4,6},{5,7},{6,4},{7,5},{8,10},{9,11},{10,... | collective-permute-start | bytes 1769480 | tf_op jit(solution)/shard_map/ppermute | solution.py:29
  121.9 67.4 %copy-start.19 = (bf16[4,96,768]{2,1,0:T(8,128)(2,1)}, bf16[4,96,768]{2,1,0:T(8,128)(2,1)S(1)}, u32[]{:S(2)}) copy-start(bf16[4,96,768]{2,1,0:T(8,128)(2,1)S(1)} %collective-permute-done.16.rest_6_) | copy-start | bytes 1769476
  121.9 40.7 %collective-permute-start.13 = (bf16[4,96,768]{2,1,0:T(8,128)(2,1)S(1)}, bf16[4,96,768]{2,1,0:T(8,128)(2,1)S(1)}, u32[]{:S(2)}, u32[]{:S(2)}) collective-permute-start(bf16[4,96,768]{2,1,0:T(8,128)(2,1)S(1)} %pad_maximum_fusion.rest_2_), channel_id=1, source_target_pairs={{0,1},{1,0},{2,3},{3,2},{4,5},{5,4},{6,7},{7,6},{8,9},{9,8},{10,11... | collective-permute-start | bytes 1769480 | tf_op jit(solution)/shard_map/ppermute | solution.py:29
  124.5 64.7 %copy-start.20 = (bf16[4,96,768]{2,1,0:T(8,128)(2,1)}, bf16[4,96,768]{2,1,0:T(8,128)(2,1)S(1)}, u32[]{:S(2)}) copy-start(bf16[4,96,768]{2,1,0:T(8,128)(2,1)S(1)} %collective-permute-done.15.rest_5_) | copy-start | bytes 1769476
  124.5 40.2 %collective-permute-start.19 = (bf16[4,96,768]{2,1,0:T(8,128)(2,1)S(1)}, bf16[4,96,768]{2,1,0:T(8,128)(2,1)}, u32[]{:S(2)}, u32[]{:S(2)}) collective-permute-start(bf16[4,96,768]{2,1,0:T(8,128)(2,1)S(1)} %collective-permute-done.15.rest_5_), channel_id=1, source_target_pairs={{0,16},{16,0},{1,17},{17,1},{2,18},{18,2},{3,19},{19,3},{4,20},{20... | collective-permute-start | bytes 1769480 | tf_op jit(solution)/shard_map/ppermute | solution.py:29
  161.4 27.9 %copy-start.21 = (bf16[4,96,768]{2,1,0:T(8,128)(2,1)}, bf16[4,96,768]{2,1,0:T(8,128)(2,1)S(1)}, u32[]{:S(2)}) copy-start(bf16[4,96,768]{2,1,0:T(8,128)(2,1)S(1)} %collective-permute-done.14.rest_4_) | copy-start | bytes 1769476
  161.4 16.3 %collective-permute-start.18 = (bf16[4,96,768]{2,1,0:T(8,128)(2,1)S(1)}, bf16[4,96,768]{2,1,0:T(8,128)(2,1)}, u32[]{:S(2)}, u32[]{:S(2)}) collective-permute-start(bf16[4,96,768]{2,1,0:T(8,128)(2,1)S(1)} %collective-permute-done.14.rest_4_), channel_id=1, source_target_pairs={{0,16},{16,0},{1,17},{17,1},{2,18},{18,2},{3,19},{19,3},{4,20},{20... | collective-permute-start | bytes 1769480 | tf_op jit(solution)/shard_map/ppermute | solution.py:29
  162.6 26.7 %copy-start.22 = (bf16[4,96,768]{2,1,0:T(8,128)(2,1)}, bf16[4,96,768]{2,1,0:T(8,128)(2,1)S(1)}, u32[]{:S(2)}) copy-start(bf16[4,96,768]{2,1,0:T(8,128)(2,1)S(1)} %collective-permute-done.13.rest_3_) | copy-start | bytes 1769476
  162.6 26.7 %collective-permute-start.17 = (bf16[4,96,768]{2,1,0:T(8,128)(2,1)S(1)}, bf16[4,96,768]{2,1,0:T(8,128)(2,1)}, u32[]{:S(2)}, u32[]{:S(2)}) collective-permute-start(bf16[4,96,768]{2,1,0:T(8,128)(2,1)S(1)} %collective-permute-done.13.rest_3_), channel_id=1, source_target_pairs={{0,16},{16,0},{1,17},{17,1},{2,18},{18,2},{3,19},{19,3},{4,20},{20... | collective-permute-start | bytes 1769480 | tf_op jit(solution)/shard_map/ppermute | solution.py:29
  203.0 13.8 %copy-start = (bf16[2,2,640,384]{3,2,1,0:T(8,128)(2,1)S(1)}, bf16[2,2,640,384]{3,2,1,0:T(8,128)(2,1)}, u32[]{:S(2)}) copy-start(bf16[2,2,640,384]{3,2,1,0:T(8,128)(2,1)} %shard_map.85) | copy-start | bytes 5898244
  219.9 6.5 %copy-start.9 = (bf16[96,1152]{1,0:T(8,128)(2,1)S(1)}, bf16[96,1152]{1,0:T(8,128)(2,1)}, u32[]{:S(2)}) copy-start(bf16[96,1152]{1,0:T(8,128)(2,1)} %copy-done.8) | copy-start | bytes 663556
  219.9 6.5 %copy-start.11 = (bf16[96,1152]{1,0:T(8,128)(2,1)S(1)}, bf16[96,1152]{1,0:T(8,128)(2,1)}, u32[]{:S(2)}) copy-start(bf16[96,1152]{1,0:T(8,128)(2,1)} %copy-done.10) | copy-start | bytes 663556
  219.9 6.5 %copy-start.13 = (bf16[96,1152]{1,0:T(8,128)(2,1)S(1)}, bf16[96,1152]{1,0:T(8,128)(2,1)}, u32[]{:S(2)}) copy-start(bf16[96,1152]{1,0:T(8,128)(2,1)} %copy-done.12) | copy-start | bytes 663556
  222.1 54.7 %copy-start.18 = (s32[12,3]{0,1:T(4,128)S(1)}, s32[12,3]{0,1:T(4,128)}, u32[]{:S(2)}) copy-start(s32[12,3]{0,1:T(4,128)} %param.14) | copy-start | bytes 436
  222.1 80.0 %collective-permute-start.21 = (bf16[2,4,160,384]{3,2,0,1:T(8,128)(2,1)}, bf16[2,4,160,384]{3,2,0,1:T(8,128)(2,1)S(1)}, u32[]{:S(2)}, u32[]{:S(2)}) collective-permute-start(bf16[2,4,160,384]{3,2,0,1:T(8,128)(2,1)} %copy.29), channel_id=1, source_target_pairs={{1,2},{2,1},{5,6},{6,5},{9,10},{10,9},{13,14},{14,13},{17,18},{18,... | collective-permute-start | bytes 2949128 | tf_op jit(solution)/shard_map/ppermute | solution.py:35
  222.9 80.2 %collective-permute-start.20 = (bf16[2,4,160,384]{3,2,0,1:T(8,128)(2,1)}, bf16[2,4,160,384]{3,2,0,1:T(8,128)(2,1)}, u32[]{:S(2)}, u32[]{:S(2)}) collective-permute-start(bf16[2,4,160,384]{3,2,0,1:T(8,128)(2,1)} %copy.28), channel_id=1, source_target_pairs={{0,1},{2,3},{1,0},{3,2},{4,5},{6,7},{5,4},{7,6},{8,9},{10,11},{9,8... | collective-permute-start | bytes 2949128 | tf_op jit(solution)/shard_map/ppermute | solution.py:35
  226.3 77.8 %collective-permute-start.22 = (bf16[2,4,160,384]{3,2,0,1:T(8,128)(2,1)}, bf16[2,4,160,384]{3,2,0,1:T(8,128)(2,1)}, u32[]{:S(2)}, u32[]{:S(2)}) collective-permute-start(bf16[2,4,160,384]{3,2,0,1:T(8,128)(2,1)} %copy.30), channel_id=1, source_target_pairs={{0,1},{2,3},{1,0},{3,2},{4,5},{6,7},{5,4},{7,6},{8,9},{10,11},{9,8... | collective-permute-start | bytes 2949128 | tf_op jit(solution)/shard_map/ppermute | solution.py:35
  226.5 79.8 %copy-start.1 = (bf16[4,96,384]{2,1,0:T(8,128)(2,1)}, bf16[4,96,384]{2,1,0:T(8,128)(2,1)S(1)}, u32[]{:S(2)}) copy-start(bf16[4,96,384]{2,1,0:T(8,128)(2,1)S(1)} %pad_maximum_fusion.4.rest_2_) | copy-start | bytes 884740
  226.5 49.6 %collective-permute-start.7 = (bf16[4,96,384]{2,1,0:T(8,128)(2,1)S(1)}, bf16[4,96,384]{2,1,0:T(8,128)(2,1)S(1)}, u32[]{:S(2)}, u32[]{:S(2)}) collective-permute-start(bf16[4,96,384]{2,1,0:T(8,128)(2,1)S(1)} %pad_maximum_fusion.4.rest_2_), channel_id=1, source_target_pairs={{0,3},{1,2},{2,1},{3,0},{4,7},{5,6},{6,5},{7,4},{8,11},{9,10},{10,... | collective-permute-start | bytes 884744 | tf_op jit(solution)/shard_map/ppermute | solution.py:29
  229.0 77.3 %collective-permute-start.23 = (bf16[2,4,160,384]{3,2,0,1:T(8,128)(2,1)}, bf16[2,4,160,384]{3,2,0,1:T(8,128)(2,1)}, u32[]{:S(2)}, u32[]{:S(2)}) collective-permute-start(bf16[2,4,160,384]{3,2,0,1:T(8,128)(2,1)} %copy.31), channel_id=1, source_target_pairs={{1,2},{2,1},{5,6},{6,5},{9,10},{10,9},{13,14},{14,13},{17,18},{18,... | collective-permute-start | bytes 2949128 | tf_op jit(solution)/shard_map/ppermute | solution.py:35
  276.7 17.0 %collective-permute-start.6 = (bf16[4,96,384]{2,1,0:T(8,128)(2,1)S(1)}, bf16[4,96,384]{2,1,0:T(8,128)(2,1)}, u32[]{:S(2)}, u32[]{:S(2)}) collective-permute-start(bf16[4,96,384]{2,1,0:T(8,128)(2,1)S(1)} %pad_maximum_fusion.4.rest_2_), channel_id=1, source_target_pairs={{0,2},{1,3},{2,0},{3,1},{4,6},{5,7},{6,4},{7,5},{8,10},{9,11},{10,... | collective-permute-start | bytes 884744 | tf_op jit(solution)/shard_map/ppermute | solution.py:29
  293.7 7.4 %collective-permute-start.5 = (bf16[4,96,384]{2,1,0:T(8,128)(2,1)S(1)}, bf16[4,96,384]{2,1,0:T(8,128)(2,1)}, u32[]{:S(2)}, u32[]{:S(2)}) collective-permute-start(bf16[4,96,384]{2,1,0:T(8,128)(2,1)S(1)} %pad_maximum_fusion.4.rest_2_), channel_id=1, source_target_pairs={{0,1},{1,0},{2,3},{3,2},{4,5},{5,4},{6,7},{7,6},{8,9},{9,8},{10,11... | collective-permute-start | bytes 884744 | tf_op jit(solution)/shard_map/ppermute | solution.py:29
  301.1 9.9 %collective-permute-start.8 = (bf16[4,96,384]{2,1,0:T(8,128)(2,1)S(1)}, bf16[4,96,384]{2,1,0:T(8,128)(2,1)S(1)}, u32[]{:S(2)}, u32[]{:S(2)}) collective-permute-start(bf16[4,96,384]{2,1,0:T(8,128)(2,1)S(1)} %pad_maximum_fusion.4.rest_2_), channel_id=1, source_target_pairs={{0,16},{16,0},{1,17},{17,1},{2,18},{18,2},{3,19},{19,3},{4,20},{20... | collective-permute-start | bytes 884744 | tf_op jit(solution)/shard_map/ppermute | solution.py:29
  302.1 15.3 %collective-permute-start.11 = (bf16[4,96,384]{2,1,0:T(8,128)(2,1)}, bf16[4,96,384]{2,1,0:T(8,128)(2,1)S(1)}, u32[]{:S(2)}, u32[]{:S(2)}) collective-permute-start(bf16[4,96,384]{2,1,0:T(8,128)(2,1)} %copy-done.2), channel_id=1, source_target_pairs={{0,16},{16,0},{1,17},{17,1},{2,18},{18,2},{3,19},{19,3},{4,20},{20... | collective-permute-start | bytes 884744 | tf_op jit(solution)/shard_map/ppermute | solution.py:29
  303.1 20.6 %collective-permute-start.10 = (bf16[4,96,384]{2,1,0:T(8,128)(2,1)}, bf16[4,96,384]{2,1,0:T(8,128)(2,1)S(1)}, u32[]{:S(2)}, u32[]{:S(2)}) collective-permute-start(bf16[4,96,384]{2,1,0:T(8,128)(2,1)} %collective-permute-done.6.rest_4_), channel_id=1, source_target_pairs={{0,16},{16,0},{1,17},{17,1},{2,18},{18,2},{3,19},{19,3},{4,20},{20... | collective-permute-start | bytes 884744 | tf_op jit(solution)/shard_map/ppermute | solution.py:29
  304.1 25.9 %collective-permute-start.9 = (bf16[4,96,384]{2,1,0:T(8,128)(2,1)}, bf16[4,96,384]{2,1,0:T(8,128)(2,1)S(1)}, u32[]{:S(2)}, u32[]{:S(2)}) collective-permute-start(bf16[4,96,384]{2,1,0:T(8,128)(2,1)} %collective-permute-done.5.rest_3_), channel_id=1, source_target_pairs={{0,16},{16,0},{1,17},{17,1},{2,18},{18,2},{3,19},{19,3},{4,20},{20... | collective-permute-start | bytes 884744 | tf_op jit(solution)/shard_map/ppermute | solution.py:29
  306.3 54.8 %collective-permute-start.24 = (bf16[2,320,384]{2,1,0:T(8,128)(2,1)S(1)}, bf16[2,320,384]{2,1,0:T(8,128)(2,1)S(1)}, u32[]{:S(2)}, u32[]{:S(2)}) collective-permute-start(bf16[2,320,384]{2,1,0:T(8,128)(2,1)S(1)} %fusion), channel_id=1, source_target_pairs={{0,16},{16,0},{1,17},{17,1},{2,18},{18,2},{3,19},{19,3},{4,20},{20... | collective-permute-start | bytes 1474568 | tf_op jit(solution)/shard_map/ppermute | solution.py:35
  311.0 19.0 %copy-start.3 = (bf16[4,96,384]{2,1,0:T(8,128)(2,1)}, bf16[4,96,384]{2,1,0:T(8,128)(2,1)S(1)}, u32[]{:S(2)}) copy-start(bf16[4,96,384]{2,1,0:T(8,128)(2,1)S(1)} %collective-permute-done.8.rest_6_) | copy-start | bytes 884740
  311.1 50.1 %collective-permute-start.25 = (bf16[2,2,160,384]{3,2,1,0:T(8,128)(2,1)S(1)}, bf16[2,2,160,384]{3,2,1,0:T(8,128)(2,1)S(1)}, u32[]{:S(2)}, u32[]{:S(2)}) collective-permute-start(bf16[2,2,160,384]{3,2,1,0:T(8,128)(2,1)S(1)} %pad_maximum_fusion.3), channel_id=1, source_target_pairs={{0,16},{16,0},{1,17},{17,1},{2,18},{18,2},{3,19},{19,3},{4,20},{20... | collective-permute-start | bytes 1474568 | tf_op jit(solution)/shard_map/ppermute | solution.py:35
  317.4 12.6 %copy-start.4 = (bf16[4,96,384]{2,1,0:T(8,128)(2,1)}, bf16[4,96,384]{2,1,0:T(8,128)(2,1)S(1)}, u32[]{:S(2)}) copy-start(bf16[4,96,384]{2,1,0:T(8,128)(2,1)S(1)} %collective-permute-done.11.rest_9_) | copy-start | bytes 884740
  323.7 6.3 %copy-start.5 = (bf16[4,96,384]{2,1,0:T(8,128)(2,1)}, bf16[4,96,384]{2,1,0:T(8,128)(2,1)S(1)}, u32[]{:S(2)}) copy-start(bf16[4,96,384]{2,1,0:T(8,128)(2,1)S(1)} %collective-permute-done.10.rest_8_) | copy-start | bytes 884740
  361.1 2.0 copy-start.23
  397.2 13.6 %collective-permute-start.27 = (bf16[640,384]{1,0:T(8,128)(2,1)S(1)}, bf16[640,384]{1,0:T(8,128)(2,1)S(1)}, u32[]{:S(2)}, u32[]{:S(2)}) collective-permute-start(bf16[640,384]{1,0:T(8,128)(2,1)S(1)} %bitcast.88), channel_id=1, source_target_pairs={{0,8},{4,12},{8,0},{12,4},{1,9},{5,13},{9,1},{13,5},{2,10},{6,14},... | collective-permute-start | bytes 1474568 | tf_op jit(solution)/shard_map/ppermute | solution.py:29
  397.2 16.9 %collective-permute-start.28 = (bf16[640,384]{1,0:T(8,128)(2,1)S(1)}, bf16[640,384]{1,0:T(8,128)(2,1)S(1)}, u32[]{:S(2)}, u32[]{:S(2)}) collective-permute-start(bf16[640,384]{1,0:T(8,128)(2,1)S(1)} %bitcast.87), channel_id=1, source_target_pairs={{0,12},{4,8},{8,4},{12,0},{1,13},{5,9},{9,5},{13,1},{2,14},{6,10},... | collective-permute-start | bytes 1474568 | tf_op jit(solution)/shard_map/ppermute | solution.py:29
  397.2 16.9 %collective-permute-start.26 = (bf16[640,384]{1,0:T(8,128)(2,1)S(1)}, bf16[640,384]{1,0:T(8,128)(2,1)S(1)}, u32[]{:S(2)}, u32[]{:S(2)}) collective-permute-start(bf16[640,384]{1,0:T(8,128)(2,1)S(1)} %bitcast.86), channel_id=1, source_target_pairs={{0,4},{4,0},{8,12},{12,8},{1,5},{5,1},{9,13},{13,9},{2,6},{6,2},{1... | collective-permute-start | bytes 1474568 | tf_op jit(solution)/shard_map/ppermute | solution.py:29
  410.8 3.3 copy-start.15
  (6 other events, 5.9 us)
